TPU v7x, 128 devices: a whole 4x4x4 slice. The times are simulated.
128 devices in a mesh: depth: 8 (over y, core), tile: 16 (over z, x).
Axes of the slice: x: 4, y: 4, z: 4, core: 2. Of those that a mesh axis runs over, the one named last changes fastest.
Arguments:
- velocity: float32 [3, 256, 256, 1024], P(None, 'depth', 'tile'), may hold values from -6 to 6
- sigma_table: float32 [16], replicated, may hold values from 0.5 to 6
- color_table: float32 [3, 16], replicated, may hold values from 0.05 to 1
Outputs:
- image: float32 [4, 256, 1024], P(None, 'tile', 'depth')
All inputs are finite; a program needn't handle non-finite values.
Results may differ from a plain program's by a relative error of at most 0.0003.
Values sent between devices are 32-bit elements; how exact they have to be, the bound alone decides.
No kernel may reach another device: no remote copies, remote signals or barrier semaphores. Data moves between devices by JAX's collectives and lax.ppermute only.
A program may use at most 128 MiB of HBM per device.

v0:
```python
import functools

import jax
import jax.numpy as jnp
from jax import lax
from jax.experimental import pallas as pl
from jax.experimental.pallas import tpu as pltpu
from jax.sharding import PartitionSpec as P

F32 = jnp.float32
VMEM_LIMIT = 40 * 1024 * 1024
QSCALE = -1.0 / 1152.0


def shift_up(count):
    return [(i, i + 1) for i in range(count - 1)]


def shift_down(count):
    return [(i + 1, i) for i in range(count - 1)]


def pack_kernel(v_ref, up_ref, down_ref, zup_ref, zdown_ref):
    zdown_ref[...] = v_ref[:, 0:2]
    zup_ref[...] = v_ref[:, 30:32]
    row = lax.broadcasted_iota(jnp.int32, (8, 1024), 0)
    for quarter in range(4):
        for zz in range(8):
            z = quarter * 8 + zz
            low = v_ref[0, z, 0:8, :]
            high = v_ref[0, z, 8:16, :]
            up = jnp.where(row == 6, high - 8.0 * pltpu.roll(high, 7, 0), high)
            down = jnp.where(row == 0, -low, 8.0 * pltpu.roll(low, 1, 0) - low)
            up_ref[0, zz, 2 * quarter : 2 * quarter + 2, :] = up[6:8]
            down_ref[0, zz, 2 * quarter : 2 * quarter + 2, :] = down[0:2]


def pack(velocity):
    comps, depth, width, length = velocity.shape
    ends = jax.ShapeDtypeStruct((comps, 8, 8, length), F32)
    layers = jax.ShapeDtypeStruct((comps, 2, width, length), F32)
    block = lambda *shape: pl.BlockSpec((1,) + shape, lambda c: (c, 0, 0, 0))
    return pl.pallas_call(
        pack_kernel,
        grid=(comps,),
        in_specs=[block(depth, width, length)],
        out_specs=[block(8, 8, length)] * 2 + [block(2, width, length)] * 2,
        out_shape=[ends, ends, layers, layers],
        compiler_params=pltpu.CompilerParams(vmem_limit_bytes=VMEM_LIMIT),
        cost_estimate=pl.CostEstimate(flops=2000000, bytes_accessed=9000000, transcendentals=0),
        name="pack",
    )(velocity)


def lookup(qcrit, tables):
    pos = 7.5 * jnp.tanh(qcrit) + 7.5
    index = jnp.minimum(pos.astype(jnp.int32), 14)
    base = [jnp.take_along_axis(t, index, axis=1, mode="promise_in_bounds") for t in tables]
    vals = [base[k] + base[k + 4] * pos for k in range(4)]
    return jnp.exp(vals[0]), vals[1:]


def composite(carry, step, colors):
    trans, shades = carry
    after = trans * step
    weight = trans - after
    return after, [s + weight * c for s, c in zip(shades, colors)]


def main_kernel(v_hbm, zlo_hbm, zhi_hbm, tab_ref, comp_ref, edge_ref, buf, sems):
    j = pl.program_id(0)

    def copies(k):
        lanes = pl.ds(pl.multiple_of(k * 128, 128), 128)
        inner = pl.ds(pl.multiple_of((k + 1) * 128, 128), 128)
        return [
            pltpu.make_async_copy(v_hbm.at[:, :, :, lanes], buf.at[:, 2:34, :, inner], sems.at[0, k]),
            pltpu.make_async_copy(zlo_hbm.at[:, :, :, lanes], buf.at[:, 0:2, :, inner], sems.at[1, k]),
            pltpu.make_async_copy(zhi_hbm.at[:, :, :, lanes], buf.at[:, 34:36, :, inner], sems.at[2, k]),
        ]

    @pl.when(j == 0)
    def _():
        for k in range(8):
            for copy in copies(k):
                copy.start()
        zeros = jnp.zeros((3, 36, 16, 128), F32)
        buf[:, :, :, 0:128] = zeros
        buf[:, :, :, 9 * 128 : 10 * 128] = zeros
        for copy in copies(0):
            copy.wait()

    @pl.when(j < 7)
    def _():
        for copy in copies(j + 1):
            copy.wait()

    row = lax.broadcasted_iota(jnp.int32, (16, 128), 0)
    lane = lax.broadcasted_iota(jnp.int32, (16, 128), 1)
    tables = [jnp.broadcast_to(tab_ref[k : k + 1, :], (16, 128)) for k in range(8)]
    left = pl.ds(pl.multiple_of(j * 128, 128), 128)
    mid = pl.ds(pl.multiple_of(j * 128 + 128, 128), 128)
    right = pl.ds(pl.multiple_of(j * 128 + 256, 128), 128)

    def layer(quarter, zz, carry):
        z = quarter * 8 + zz
        dz, dx, dy = [], [], []
        for c in range(3):
            center = buf[c, z + 2, :, mid]
            dz.append(8.0 * (buf[c, z + 3, :, mid] - buf[c, z + 1, :, mid]) - (buf[c, z + 4, :, mid] - buf[c, z, :, mid]))
            p1 = jnp.where(row < 15, pltpu.roll(center, 15, 0), 0.0)
            m1 = jnp.where(row > 0, pltpu.roll(center, 1, 0), 0.0)
            p2 = jnp.where(row < 14, pltpu.roll(center, 14, 0), 0.0)
            m2 = jnp.where(row > 1, pltpu.roll(center, 2, 0), 0.0)
            dx.append(8.0 * (p1 - m1) - (p2 - m2))
            lo = buf[c, z + 2, :, left]
            hi = buf[c, z + 2, :, right]
            p1 = pltpu.roll(jnp.where(lane < 1, hi, center), 127, 1)
            m1 = pltpu.roll(jnp.where(lane > 126, lo, center), 1, 1)
            p2 = pltpu.roll(jnp.where(lane < 2, hi, center), 126, 1)
            m2 = pltpu.roll(jnp.where(lane > 125, lo, center), 2, 1)
            dy.append(8.0 * (p1 - m1) - (p2 - m2))
        cross = dz[1] * dx[0] + dz[2] * dy[0] + dx[2] * dy[1]
        total = dz[0] * dz[0] + dx[1] * dx[1] + dy[2] * dy[2] + 2.0 * cross
        for e, value in enumerate((total, 2.0 * dz[1], 2.0 * dx[1], 2.0 * dy[1])):
            edge_ref[e, 0, zz, 2 * quarter : 2 * quarter + 2, :] = value[0:2]
            edge_ref[e, 1, zz, 2 * quarter : 2 * quarter + 2, :] = value[14:16]
        step, colors = lookup(QSCALE * total, tables)
        return composite(carry, step, colors)

    carry = (jnp.ones((16, 128), F32), [jnp.zeros((16, 128), F32)] * 3)
    for quarter in range(4):
        carry = lax.fori_loop(0, 8, functools.partial(layer, quarter), carry)
    for c in range(3):
        comp_ref[c] = carry[1][c]
    comp_ref[3] = carry[0]


def main_pass(velocity, before, after, table):
    comps, depth, width, length = velocity.shape
    hbm = pl.BlockSpec(memory_space=pl.ANY)
    return pl.pallas_call(
        main_kernel,
        grid=(8,),
        in_specs=[hbm, hbm, hbm, pl.BlockSpec((8, 128), lambda j: (0, 0))],
        out_specs=[
            pl.BlockSpec((4, width, 128), lambda j: (0, 0, j)),
            pl.BlockSpec((4, 2, 8, 8, 128), lambda j: (0, 0, 0, 0, j)),
        ],
        out_shape=[
            jax.ShapeDtypeStruct((4, width, length), F32),
            jax.ShapeDtypeStruct((4, 2, 8, 8, length), F32),
        ],
        scratch_shapes=[pltpu.VMEM((comps, depth + 4, width, length + 256), F32), pltpu.SemaphoreType.DMA((3, 8))],
        compiler_params=pltpu.CompilerParams(vmem_limit_bytes=VMEM_LIMIT),
        cost_estimate=pl.CostEstimate(flops=60000000, bytes_accessed=10000000, transcendentals=1000000),
        name="main_pass",
    )(velocity, before, after, table)


def edge_kernel(edge_ref, lo_ref, hi_ref, comp_ref, tab_ref, out_ref):
    tables = [jnp.broadcast_to(tab_ref[k : k + 1, :], (8, 128)) for k in range(8)]
    for half in range(2):
        lanes = slice(half * 128, half * 128 + 128)
        out_ref[half] = comp_ref[:, :, lanes]
        for side, halo_ref in enumerate((lo_ref, hi_ref)):
            carry = (jnp.ones((8, 128), F32), [jnp.zeros((8, 128), F32)] * 3)
            for zz in range(8):
                part, by_z, by_x, by_y = [edge_ref[e, side, zz, :, lanes] for e in range(4)]
                hz, hx, hy = [halo_ref[c, zz, :, lanes] for c in range(3)]
                total = part + by_z * hz + by_y * hy + hx * (by_x + hx)
                step, colors = lookup(QSCALE * total, tables)
                carry = composite(carry, step, colors)
            trans, shades = carry
            for _ in range(2):
                back = 2 if _ == 0 else 4
                behind = pltpu.roll(trans, 8 - back, 0)
                shades = [s + trans * pltpu.roll(s, 8 - back, 0) for s in shades]
                trans = trans * behind
            start = 14 * side
            for c in range(3):
                out_ref[half, c, start : start + 2, :] = shades[c][0:2]
            out_ref[half, 3, start : start + 2, :] = trans[0:2]


def edge_pass(edge, lo, hi, comp, table):
    length = comp.shape[2]
    width = comp.shape[1]
    halo = pl.BlockSpec((3, 8, 8, 256), lambda j: (0, 0, 0, j))
    return pl.pallas_call(
        edge_kernel,
        grid=(length // 256,),
        in_specs=[
            pl.BlockSpec((4, 2, 8, 8, 256), lambda j: (0, 0, 0, 0, j)),
            halo,
            halo,
            pl.BlockSpec((4, width, 256), lambda j: (0, 0, j)),
            pl.BlockSpec((8, 128), lambda j: (0, 0)),
        ],
        out_specs=pl.BlockSpec((2, 4, width, 128), lambda j: (j, 0, 0, 0)),
        out_shape=jax.ShapeDtypeStruct((8, 4, width, 128), F32),
        compiler_params=pltpu.CompilerParams(vmem_limit_bytes=VMEM_LIMIT),
        cost_estimate=pl.CostEstimate(flops=10000000, bytes_accessed=4000000, transcendentals=300000),
        name="edge_pass",
    )(edge, lo, hi, comp, table)


def over_kernel(parts_ref, out_ref):
    shades = [parts_ref[7, c] for c in range(3)]
    trans = parts_ref[7, 3]
    for layer in range(6, -1, -1):
        front = parts_ref[layer, 3]
        shades = [parts_ref[layer, c] + front * s for c, s in enumerate(shades)]
        trans = trans * front
    for c in range(3):
        out_ref[c] = shades[c]
    out_ref[3] = trans


def over(parts):
    return pl.pallas_call(
        over_kernel,
        out_shape=jax.ShapeDtypeStruct(parts.shape[1:], F32),
        name="over",
    )(parts)


def make_table(sigma_table, color_table, depth_total):
    values = jnp.concatenate([sigma_table[None] * (-1.0 / depth_total), color_table], axis=0)
    slopes = values[:, 1:] - values[:, :-1]
    starts = values[:, :-1] - slopes * jnp.arange(15, dtype=F32)
    table = jnp.concatenate([starts, slopes], axis=0)
    return jnp.pad(table, ((0, 0), (0, 113)))


def local(velocity, sigma_table, color_table):
    layers, tiles = lax.axis_size("depth"), lax.axis_size("tile")
    table = make_table(sigma_table, color_table, velocity.shape[1] * layers)
    up, down, zup, zdown = pack(velocity)
    lo = lax.ppermute(up, "tile", shift_up(tiles))
    hi = lax.ppermute(down, "tile", shift_down(tiles))
    before = lax.ppermute(zup, "depth", shift_up(layers))
    after = lax.ppermute(zdown, "depth", shift_down(layers))
    comp, edge = main_pass(velocity, before, after, table)
    pieces = edge_pass(edge, lo, hi, comp, table)
    received = lax.all_to_all(pieces, "depth", split_axis=0, concat_axis=0, tiled=True)
    return over(received)


def solution(mesh):
    return jax.shard_map(
        local,
        mesh=mesh,
        in_specs=(P(None, "depth", "tile", None), P(), P()),
        out_specs=P(None, "tile", "depth"),
        check_vma=False,
    )
```

profile of v0, /device:TPU:32, one launch (start us, length us, event | category | flops | bytes accessed | tf_op | source)
XLA Modules:
  0.0 96.6 jit_solution(17379040524819680775)
XLA Ops:
  0.0 0.0 copy-start
  0.0 2.8 %copy-done = f32[3,32,16,1024]{3,2,1,0:T(8,128)S(1)} copy-done((f32[3,32,16,1024]{3,2,1,0:T(8,128)S(1)}, f32[3,32,16,1024]{3,2,1,0:T(8,128)}, u32[]{:S(2)}) %copy-start) | copy-done | bytes 6291480
  2.8 0.0 copy-start.2
  2.8 0.0 copy-start.1
  2.8 1.1 %pack.1 = (f32[3,8,8,1024]{3,2,1,0:T(8,128)S(1)}, f32[3,8,8,1024]{3,2,1,0:T(8,128)S(1)}, f32[3,2,16,1024]{3,2,1,0:T(8,128)S(1)}, f32[3,2,16,1024]{3,2,1,0:T(8,128)S(1)}) custom-call(f32[3,32,16,1024]{3,2,1,0:T(8,128)S(1)} %copy-done), custom_call_target="tpu_custom_call" | custom-call | flops 2000000 | bytes 9000000 | tf_op jit(solution)/shard_map/pack/pallas_call | solution.py:43
  3.9 3.4 %collective-permute-start.2 = (f32[3,8,8,1024]{3,2,1,0:T(8,128)S(1)}, f32[3,8,8,1024]{3,2,1,0:T(8,128)S(1)}, u32[]{:S(2)}, u32[]{:S(2)}) collective-permute-start(f32[3,8,8,1024]{3,2,1,0:T(8,128)S(1)} %get-tuple-element.14), channel_id=1, source_target_pairs={{0,1},{1,2},{2,3},{3,4},{4,5},{5,6},{6,7},{7,8},{8,9},{9,10},{10,1... | collective-permute-start | bytes 2359304 | tf_op jit(solution)/shard_map/ppermute | solution.py:240
  7.3 4.6 %collective-permute-start.3 = (f32[3,8,8,1024]{3,2,1,0:T(8,128)S(1)}, f32[3,8,8,1024]{3,2,1,0:T(8,128)S(1)}, u32[]{:S(2)}, u32[]{:S(2)}) collective-permute-start(f32[3,8,8,1024]{3,2,1,0:T(8,128)S(1)} %get-tuple-element.15), channel_id=1, source_target_pairs={{1,0},{2,1},{3,2},{4,3},{5,4},{6,5},{7,6},{8,7},{9,8},{10,9},{11,1... | collective-permute-start | bytes 2359304 | tf_op jit(solution)/shard_map/ppermute | solution.py:241
  11.9 1.3 %collective-permute-start = (f32[3,2,16,1024]{3,2,1,0:T(8,128)S(1)}, f32[3,2,16,1024]{3,2,1,0:T(8,128)S(1)}, u32[]{:S(2)}, u32[]{:S(2)}) collective-permute-start(f32[3,2,16,1024]{3,2,1,0:T(8,128)S(1)} %get-tuple-element.11), channel_id=1, source_target_pairs={{0,16},{16,32},{32,48},{48,64},{64,80},{80,96},{96,112},{1,17},{17... | collective-permute-start | bytes 1179656 | tf_op jit(solution)/shard_map/ppermute | solution.py:242
  13.2 1.3 %collective-permute-start.1 = (f32[3,2,16,1024]{3,2,1,0:T(8,128)S(1)}, f32[3,2,16,1024]{3,2,1,0:T(8,128)S(1)}, u32[]{:S(2)}, u32[]{:S(2)}) collective-permute-start(f32[3,2,16,1024]{3,2,1,0:T(8,128)S(1)} %get-tuple-element.12), channel_id=1, source_target_pairs={{16,0},{32,16},{48,32},{64,48},{80,64},{96,80},{112,96},{17,1},{33... | collective-permute-start | bytes 1179656 | tf_op jit(solution)/shard_map/ppermute | solution.py:243
  14.5 0.0 copy-done.2
  14.5 0.0 copy-done.1
  14.6 0.1 multiply_subtract_fusion
  14.7 0.0 collective-permute-done.zlo_hbm
  14.7 4.0 %collective-permute-done.1.zhi_hbm = f32[3,2,16,1024]{3,2,1,0:T(8,128)S(1)} collective-permute-done((f32[3,2,16,1024]{3,2,1,0:T(8,128)S(1)}, f32[3,2,16,1024]{3,2,1,0:T(8,128)S(1)}, u32[]{:S(2)}, u32[]{:S(2)}) %collective-permute-start.1) | collective-permute-done | bytes 393248 | tf_op jit(solution)/shard_map/ppermute | solution.py:243
  18.6 56.6 %main_pass.1 = (f32[4,16,1024]{2,1,0:T(8,128)S(1)}, f32[4,2,8,8,1024]{4,3,2,1,0:T(8,128)S(1)}) custom-call(f32[3,32,16,1024]{3,2,1,0:T(8,128)S(1)} %copy-done, f32[3,2,16,1024]{3,2,1,0:T(8,128)S(1)} %collective-permute-done.zlo_hbm, f32[3,2,16,1024]{3,2,1,0:T(8,128)S(1)} %collective-permute-done.1.zhi_hbm, f32[8,128]{1,0:T(8,128)S(1)} %select_maximum_fusion.tab_ref), custom_call_target="tpu_custom_call" | custom-call | flops 60000000 | bytes 10000000 | tf_op jit(solution)/shard_map/main_pass/pallas_call | solution.py:142
  75.2 0.0 collective-permute-done.2.lo_ref
  75.2 0.0 collective-permute-done.3.hi_ref
  75.2 2.3 %edge_pass.1 = f32[8,4,16,128]{3,2,1,0:T(8,128)S(1)} custom-call(f32[4,2,8,8,1024]{4,3,2,1,0:T(8,128)S(1)} %get-tuple-element.13.edge_ref, f32[3,8,8,1024]{3,2,1,0:T(8,128)S(1)} %collective-permute-done.2.lo_ref, f32[3,8,8,1024]{3,2,1,0:T(8,128)S(1)} %collective-permute-done.3.hi_ref, f32[4,16,1024]{2,1,0:T(8,128)S(1)} %get-tuple-element.16.comp_ref, ...), custom_call_target="tpu_custom_call" | custom-call | flops 10000000 | bytes 4000000 | tf_op jit(solution)/shard_map/edge_pass/pallas_call | solution.py:190
  77.5 17.5 %all_to_all.5.parts_ref = f32[8,4,16,128]{3,2,1,0:T(8,128)} all-to-all(f32[8,4,16,128]{3,2,1,0:T(8,128)S(1)} %edge_pass.1), channel_id=1, replica_groups=mesh['depth'=8,'tile'=16] {'depth'}, dimensions={0} | all-to-all | bytes 524288 | tf_op jit(solution)/shard_map/all_to_all | solution.py:246
  95.0 1.6 %over.1 = f32[4,16,128]{2,1,0:T(8,128)} custom-call(f32[8,4,16,128]{3,2,1,0:T(8,128)} %all_to_all.5.parts_ref), custom_call_target="tpu_custom_call" | custom-call | tf_op jit(solution)/shard_map/over/pallas_call | solution.py:221
  (3 shorter events, 0.0 us)
Async XLA Ops:
  0.0 2.8 %copy-start = (f32[3,32,16,1024]{3,2,1,0:T(8,128)S(1)}, f32[3,32,16,1024]{3,2,1,0:T(8,128)}, u32[]{:S(2)}) copy-start(f32[3,32,16,1024]{3,2,1,0:T(8,128)} %v_hbm.1) | copy-start | bytes 18874372
  2.8 11.7 %copy-start.2 = (f32[16]{0:T(128)S(1)}, f32[16]{0:T(128)}, u32[]{:S(2)}) copy-start(f32[16]{0:T(128)} %param.4) | copy-start | bytes 196
  2.8 11.8 %copy-start.1 = (f32[3,16]{1,0:T(4,128)S(1)}, f32[3,16]{1,0:T(4,128)}, u32[]{:S(2)}) copy-start(f32[3,16]{1,0:T(4,128)} %param.5) | copy-start | bytes 580
  3.9 71.3 %collective-permute-start.2 = (f32[3,8,8,1024]{3,2,1,0:T(8,128)S(1)}, f32[3,8,8,1024]{3,2,1,0:T(8,128)S(1)}, u32[]{:S(2)}, u32[]{:S(2)}) collective-permute-start(f32[3,8,8,1024]{3,2,1,0:T(8,128)S(1)} %get-tuple-element.14), channel_id=1, source_target_pairs={{0,1},{1,2},{2,3},{3,4},{4,5},{5,6},{6,7},{7,8},{8,9},{9,10},{10,1... | collective-permute-start | bytes 2359304 | tf_op jit(solution)/shard_map/ppermute | solution.py:240
  7.3 67.9 %collective-permute-start.3 = (f32[3,8,8,1024]{3,2,1,0:T(8,128)S(1)}, f32[3,8,8,1024]{3,2,1,0:T(8,128)S(1)}, u32[]{:S(2)}, u32[]{:S(2)}) collective-permute-start(f32[3,8,8,1024]{3,2,1,0:T(8,128)S(1)} %get-tuple-element.15), channel_id=1, source_target_pairs={{1,0},{2,1},{3,2},{4,3},{5,4},{6,5},{7,6},{8,7},{9,8},{10,9},{11,1... | collective-permute-start | bytes 2359304 | tf_op jit(solution)/shard_map/ppermute | solution.py:241
  11.9 2.8 %collective-permute-start = (f32[3,2,16,1024]{3,2,1,0:T(8,128)S(1)}, f32[3,2,16,1024]{3,2,1,0:T(8,128)S(1)}, u32[]{:S(2)}, u32[]{:S(2)}) collective-permute-start(f32[3,2,16,1024]{3,2,1,0:T(8,128)S(1)} %get-tuple-element.11), channel_id=1, source_target_pairs={{0,16},{16,32},{32,48},{48,64},{64,80},{80,96},{96,112},{1,17},{17... | collective-permute-start | bytes 1179656 | tf_op jit(solution)/shard_map/ppermute | solution.py:242
  13.2 5.4 %collective-permute-start.1 = (f32[3,2,16,1024]{3,2,1,0:T(8,128)S(1)}, f32[3,2,16,1024]{3,2,1,0:T(8,128)S(1)}, u32[]{:S(2)}, u32[]{:S(2)}) collective-permute-start(f32[3,2,16,1024]{3,2,1,0:T(8,128)S(1)} %get-tuple-element.12), channel_id=1, source_target_pairs={{16,0},{32,16},{48,32},{64,48},{80,64},{96,80},{112,96},{17,1},{33... | collective-permute-start | bytes 1179656 | tf_op jit(solution)/shard_map/ppermute | solution.py:243
where the time goes:
time: 96.9 us; the launch traced here: 96.6 us
  Pallas kernels  61.6 us (64%)
  blocking collectives  17.5 us (18%)
  starting transfers between devices  10.6 us (11%)
  waiting for transfers between devices  3.97 us (4%)
  local copies, waits for them, and re-layouts  2.79 us (3%)
    pallas_call x1, Pallas kernels, main_pass(): pl.pallas_call(main_kernel, grid=(8,), in_specs=[hbm, hbm, hbm, pl.BlockS...  56.6 us
    all_to_all x1, blocking collectives, local(): lax.all_to_all(pieces, 'depth', split_axis=0, concat_axis=0, tiled=True)  17.5 us
    ppermute x1, starting transfers between devices, local(): hi = lax.ppermute(down, 'tile', shift_down(tiles))  4.55 us
    ppermute x1, waiting for transfers between devices, local(): after = lax.ppermute(zdown, 'depth', shift_down(layers))  3.96 us
    ppermute x1, starting transfers between devices, local(): lo = lax.ppermute(up, 'tile', shift_up(tiles))  3.4 us
    unnamed x6, local copies, waits for them, and re-layouts  2.79 us
    pallas_call x1, Pallas kernels, edge_pass(): pl.pallas_call(edge_kernel, grid=(length // 256,), in_specs=[pl.BlockSpec...  2.25 us
  transfers between devices with their start and end apart: 4, of which 1 were waited for; matrix products, arithmetic and copies ran while one was open for 0% of the time, Pallas kernels for 59%

commit v1 on v0

--- a/solution.py
+++ b/solution.py
@@ -52,10 +52,12 @@
     )(velocity)
 
 
-def lookup(qcrit, tables):
+def lookup(qcrit, tab_ref):
     pos = 7.5 * jnp.tanh(qcrit) + 7.5
     index = jnp.minimum(pos.astype(jnp.int32), 14)
-    base = [jnp.take_along_axis(t, index, axis=1, mode="promise_in_bounds") for t in tables]
+    low, index = index < 8, index & 7
+    pick = lambda k: jnp.take_along_axis(tab_ref[k], index, axis=0, mode="promise_in_bounds")
+    base = [jnp.where(low, pick(2 * k), pick(2 * k + 1)) for k in range(8)]
     vals = [base[k] + base[k + 4] * pos for k in range(4)]
     return jnp.exp(vals[0]), vals[1:]
 
@@ -95,26 +97,29 @@
         for copy in copies(j + 1):
             copy.wait()
 
-    row = lax.broadcasted_iota(jnp.int32, (16, 128), 0)
-    lane = lax.broadcasted_iota(jnp.int32, (16, 128), 1)
-    tables = [jnp.broadcast_to(tab_ref[k : k + 1, :], (16, 128)) for k in range(8)]
+    row = lax.broadcasted_iota(jnp.int32, (8, 128), 0)
+    lane = lax.broadcasted_iota(jnp.int32, (8, 128), 1)
     left = pl.ds(pl.multiple_of(j * 128, 128), 128)
     mid = pl.ds(pl.multiple_of(j * 128 + 128, 128), 128)
     right = pl.ds(pl.multiple_of(j * 128 + 256, 128), 128)
 
-    def layer(quarter, zz, carry):
-        z = quarter * 8 + zz
+    def layer(side, quarter, zz, z, window, carry):
+        rows = slice(8 * side, 8 * side + 8)
+        others = slice(8 - 8 * side, 16 - 8 * side)
         dz, dx, dy = [], [], []
         for c in range(3):
-            center = buf[c, z + 2, :, mid]
-            dz.append(8.0 * (buf[c, z + 3, :, mid] - buf[c, z + 1, :, mid]) - (buf[c, z + 4, :, mid] - buf[c, z, :, mid]))
-            p1 = jnp.where(row < 15, pltpu.roll(center, 15, 0), 0.0)
-            m1 = jnp.where(row > 0, pltpu.roll(center, 1, 0), 0.0)
-            p2 = jnp.where(row < 14, pltpu.roll(center, 14, 0), 0.0)
-            m2 = jnp.where(row > 1, pltpu.roll(center, 2, 0), 0.0)
+            w = window[c]
+            center = w[2]
+            dz.append(8.0 * (w[3] - w[1]) - (w[4] - w[0]))
+            other = buf[c, z + 2, others, mid]
+            above, below = (0.0, other) if side == 0 else (other, 0.0)
+            p1 = pltpu.roll(jnp.where(row < 1, below, center), 7, 0)
+            m1 = pltpu.roll(jnp.where(row > 6, above, center), 1, 0)
+            p2 = pltpu.roll(jnp.where(row < 2, below, center), 6, 0)
+            m2 = pltpu.roll(jnp.where(row > 5, above, center), 2, 0)
             dx.append(8.0 * (p1 - m1) - (p2 - m2))
-            lo = buf[c, z + 2, :, left]
-            hi = buf[c, z + 2, :, right]
+            lo = buf[c, z + 2, rows, left]
+            hi = buf[c, z + 2, rows, right]
             p1 = pltpu.roll(jnp.where(lane < 1, hi, center), 127, 1)
             m1 = pltpu.roll(jnp.where(lane > 126, lo, center), 1, 1)
             p2 = pltpu.roll(jnp.where(lane < 2, hi, center), 126, 1)
@@ -122,18 +127,25 @@
             dy.append(8.0 * (p1 - m1) - (p2 - m2))
         cross = dz[1] * dx[0] + dz[2] * dy[0] + dx[2] * dy[1]
         total = dz[0] * dz[0] + dx[1] * dx[1] + dy[2] * dy[2] + 2.0 * cross
+        ends = slice(6 * side, 6 * side + 2)
         for e, value in enumerate((total, 2.0 * dz[1], 2.0 * dx[1], 2.0 * dy[1])):
-            edge_ref[e, 0, zz, 2 * quarter : 2 * quarter + 2, :] = value[0:2]
-            edge_ref[e, 1, zz, 2 * quarter : 2 * quarter + 2, :] = value[14:16]
-        step, colors = lookup(QSCALE * total, tables)
+            edge_ref[e, side, zz, 2 * quarter : 2 * quarter + 2, :] = value[ends]
+        step, colors = lookup(QSCALE * total, tab_ref)
         return composite(carry, step, colors)
 
-    carry = (jnp.ones((16, 128), F32), [jnp.zeros((16, 128), F32)] * 3)
-    for quarter in range(4):
-        carry = lax.fori_loop(0, 8, functools.partial(layer, quarter), carry)
-    for c in range(3):
-        comp_ref[c] = carry[1][c]
-    comp_ref[3] = carry[0]
+    for side in range(2):
+        rows = slice(8 * side, 8 * side + 8)
+        zeros = jnp.zeros((8, 128), F32)
+        carry = (zeros + 1.0, [zeros] * 3)
+        for quarter in range(4):
+            first = quarter * 8
+            lines = [[buf[c, first + i, rows, mid] for i in range(12)] for c in range(3)]
+            for i in range(8):
+                window = [lines[c][i : i + 5] for c in range(3)]
+                carry = layer(side, quarter, i, first + i, window, carry)
+        for c in range(3):
+            comp_ref[c, rows, :] = carry[1][c]
+        comp_ref[3, rows, :] = carry[0]
 
 
 def main_pass(velocity, before, after, table):
@@ -142,7 +154,7 @@
     return pl.pallas_call(
         main_kernel,
         grid=(8,),
-        in_specs=[hbm, hbm, hbm, pl.BlockSpec((8, 128), lambda j: (0, 0))],
+        in_specs=[hbm, hbm, hbm, pl.BlockSpec((16, 8, 128), lambda j: (0, 0, 0))],
         out_specs=[
             pl.BlockSpec((4, width, 128), lambda j: (0, 0, j)),
             pl.BlockSpec((4, 2, 8, 8, 128), lambda j: (0, 0, 0, 0, j)),
@@ -159,45 +171,32 @@
 
 
 def edge_kernel(edge_ref, lo_ref, hi_ref, comp_ref, tab_ref, out_ref):
-    tables = [jnp.broadcast_to(tab_ref[k : k + 1, :], (8, 128)) for k in range(8)]
-    for half in range(2):
-        lanes = slice(half * 128, half * 128 + 128)
-        out_ref[half] = comp_ref[:, :, lanes]
+    for j in range(8):
+        lanes = slice(j * 128, j * 128 + 128)
+        out_ref[j] = comp_ref[:, :, lanes]
         for side, halo_ref in enumerate((lo_ref, hi_ref)):
-            carry = (jnp.ones((8, 128), F32), [jnp.zeros((8, 128), F32)] * 3)
+            zeros = jnp.zeros((8, 128), F32)
+            carry = (zeros + 1.0, [zeros] * 3)
             for zz in range(8):
                 part, by_z, by_x, by_y = [edge_ref[e, side, zz, :, lanes] for e in range(4)]
                 hz, hx, hy = [halo_ref[c, zz, :, lanes] for c in range(3)]
                 total = part + by_z * hz + by_y * hy + hx * (by_x + hx)
-                step, colors = lookup(QSCALE * total, tables)
+                step, colors = lookup(QSCALE * total, tab_ref)
                 carry = composite(carry, step, colors)
             trans, shades = carry
-            for _ in range(2):
-                back = 2 if _ == 0 else 4
-                behind = pltpu.roll(trans, 8 - back, 0)
+            for back in (2, 4):
                 shades = [s + trans * pltpu.roll(s, 8 - back, 0) for s in shades]
-                trans = trans * behind
+                trans = trans * pltpu.roll(trans, 8 - back, 0)
             start = 14 * side
             for c in range(3):
-                out_ref[half, c, start : start + 2, :] = shades[c][0:2]
-            out_ref[half, 3, start : start + 2, :] = trans[0:2]
+                out_ref[j, c, start : start + 2, :] = shades[c][0:2]
+            out_ref[j, 3, start : start + 2, :] = trans[0:2]
 
 
 def edge_pass(edge, lo, hi, comp, table):
-    length = comp.shape[2]
     width = comp.shape[1]
-    halo = pl.BlockSpec((3, 8, 8, 256), lambda j: (0, 0, 0, j))
     return pl.pallas_call(
         edge_kernel,
-        grid=(length // 256,),
-        in_specs=[
-            pl.BlockSpec((4, 2, 8, 8, 256), lambda j: (0, 0, 0, 0, j)),
-            halo,
-            halo,
-            pl.BlockSpec((4, width, 256), lambda j: (0, 0, j)),
-            pl.BlockSpec((8, 128), lambda j: (0, 0)),
-        ],
-        out_specs=pl.BlockSpec((2, 4, width, 128), lambda j: (j, 0, 0, 0)),
         out_shape=jax.ShapeDtypeStruct((8, 4, width, 128), F32),
         compiler_params=pltpu.CompilerParams(vmem_limit_bytes=VMEM_LIMIT),
         cost_estimate=pl.CostEstimate(flops=10000000, bytes_accessed=4000000, transcendentals=300000),
@@ -230,7 +229,8 @@
     slopes = values[:, 1:] - values[:, :-1]
     starts = values[:, :-1] - slopes * jnp.arange(15, dtype=F32)
     table = jnp.concatenate([starts, slopes], axis=0)
-    return jnp.pad(table, ((0, 0), (0, 113)))
+    table = jnp.pad(table, ((0, 0), (0, 1))).reshape(16, 8, 1)
+    return jnp.broadcast_to(table, (16, 8, 128))
 
 
 def local(velocity, sigma_table, color_table):

time: 96.9 us -> 54.9 us (0.57)
  Pallas kernels: 61.6 us -> 16.8 us
  local copies, waits for them, and re-layouts: 2.79 us -> 5.73 us
    pallas_call x1, Pallas kernels: 56.6 us -> 12 us  [main_pass(): pl.pallas_call(main_kernel, grid=(8,), in_specs=[hbm, hbm, hbm, pl.BlockS...]
    unnamed x6 -> x8, local copies, waits for them, and re-layouts: 2.79 us -> 5.58 us
    pallas_call x1, Pallas kernels: 2.25 us -> 1.24 us  [edge_pass(): pl.pallas_call(edge_kernel, out_shape=jax.ShapeDtypeStruct((8, 4, width,...]
  transfers between devices with their start and end apart: 4 -> 4, of which waited for: 1 -> 1; matrix products, arithmetic and copies ran while one was open for 0% -> 0% of each run, Pallas kernels for 59% -> 22%
where the time goes in v1:
time: 54.9 us; the launch traced here: 54.6 us
  blocking collectives  17.5 us (32%)
  Pallas kernels  16.8 us (31%)
  starting transfers between devices  10.5 us (19%)
  local copies, waits for them, and re-layouts  5.73 us (10%)
  waiting for transfers between devices  3.9 us (7%)
    all_to_all x1, blocking collectives, local(): lax.all_to_all(pieces, 'depth', split_axis=0, concat_axis=0, tiled=True)  17.5 us
    pallas_call x1, Pallas kernels, main_pass(): pl.pallas_call(main_kernel, grid=(8,), in_specs=[hbm, hbm, hbm, pl.BlockS...  12 us
    unnamed x8, local copies, waits for them, and re-layouts  5.58 us
    ppermute x1, starting transfers between devices, local(): hi = lax.ppermute(down, 'tile', shift_down(tiles))  4.55 us
    ppermute x1, waiting for transfers between devices, local(): after = lax.ppermute(zdown, 'depth', shift_down(layers))  3.89 us
    ppermute x1, starting transfers between devices, local(): lo = lax.ppermute(up, 'tile', shift_up(tiles))  3.39 us
    pallas_call x1, Pallas kernels, pack(): pl.pallas_call(pack_kernel, grid=(comps,), in_specs=[block(depth, width,...  1.9 us
    pallas_call x1, Pallas kernels, over(): pl.pallas_call(over_kernel, out_shape=jax.ShapeDtypeStruct(parts.shape[1:...  1.58 us
  transfers between devices with their start and end apart: 4, of which 1 were waited for; matrix products, arithmetic and copies ran while one was open for 0% of the time, Pallas kernels for 22%

profile of v1, /device:TPU:32, one launch (start us, length us, event | category | flops | bytes accessed | tf_op | source)
XLA Modules:
  0.0 54.6 jit_solution(7401340004352392605)
XLA Ops:
  0.0 0.0 copy-start
  0.0 2.8 %copy-done = f32[3,32,16,1024]{3,2,1,0:T(8,128)S(1)} copy-done((f32[3,32,16,1024]{3,2,1,0:T(8,128)S(1)}, f32[3,32,16,1024]{3,2,1,0:T(8,128)}, u32[]{:S(2)}) %copy-start) | copy-done | bytes 6291480
  2.8 0.0 copy-start.3
  2.8 0.0 copy-start.2
  2.8 1.9 %pack.1 = (f32[3,8,8,1024]{3,2,1,0:T(8,128)}, f32[3,8,8,1024]{3,2,1,0:T(8,128)S(1)}, f32[3,2,16,1024]{3,2,1,0:T(8,128)}, f32[3,2,16,1024]{3,2,1,0:T(8,128)S(1)}) custom-call(f32[3,32,16,1024]{3,2,1,0:T(8,128)S(1)} %copy-done), custom_call_target="tpu_custom_call" | custom-call | flops 2000000 | bytes 9000000 | tf_op jit(solution)/shard_map/pack/pallas_call | solution.py:43
  4.7 3.4 %collective-permute-start.2 = (f32[3,8,8,1024]{3,2,1,0:T(8,128)}, f32[3,8,8,1024]{3,2,1,0:T(8,128)S(1)}, u32[]{:S(2)}, u32[]{:S(2)}) collective-permute-start(f32[3,8,8,1024]{3,2,1,0:T(8,128)} %get-tuple-element.14), channel_id=1, source_target_pairs={{0,1},{1,2},{2,3},{3,4},{4,5},{5,6},{6,7},{7,8},{8,9},{9,10},{10,1... | collective-permute-start | bytes 2359304 | tf_op jit(solution)/shard_map/ppermute | solution.py:240
  8.1 4.6 %collective-permute-start.3 = (f32[3,8,8,1024]{3,2,1,0:T(8,128)S(1)}, f32[3,8,8,1024]{3,2,1,0:T(8,128)S(1)}, u32[]{:S(2)}, u32[]{:S(2)}) collective-permute-start(f32[3,8,8,1024]{3,2,1,0:T(8,128)S(1)} %get-tuple-element.15), channel_id=1, source_target_pairs={{1,0},{2,1},{3,2},{4,3},{5,4},{6,5},{7,6},{8,7},{9,8},{10,9},{11,1... | collective-permute-start | bytes 2359304 | tf_op jit(solution)/shard_map/ppermute | solution.py:241
  12.6 1.3 %collective-permute-start = (f32[3,2,16,1024]{3,2,1,0:T(8,128)}, f32[3,2,16,1024]{3,2,1,0:T(8,128)S(1)}, u32[]{:S(2)}, u32[]{:S(2)}) collective-permute-start(f32[3,2,16,1024]{3,2,1,0:T(8,128)} %get-tuple-element.11), channel_id=1, source_target_pairs={{0,16},{16,32},{32,48},{48,64},{64,80},{80,96},{96,112},{1,17},{17... | collective-permute-start | bytes 1179656 | tf_op jit(solution)/shard_map/ppermute | solution.py:242
  14.0 1.3 %collective-permute-start.1 = (f32[3,2,16,1024]{3,2,1,0:T(8,128)S(1)}, f32[3,2,16,1024]{3,2,1,0:T(8,128)S(1)}, u32[]{:S(2)}, u32[]{:S(2)}) collective-permute-start(f32[3,2,16,1024]{3,2,1,0:T(8,128)S(1)} %get-tuple-element.12), channel_id=1, source_target_pairs={{16,0},{32,16},{48,32},{64,48},{80,64},{96,80},{112,96},{17,1},{33... | collective-permute-start | bytes 1179656 | tf_op jit(solution)/shard_map/ppermute | solution.py:243
  15.3 0.0 copy-done.3
  15.3 0.0 copy-done.2
  15.3 0.1 multiply_subtract_fusion
  15.4 0.1 broadcast_in_dim.4
  15.5 0.0 collective-permute-done.zlo_hbm
  15.5 3.9 %collective-permute-done.1.zhi_hbm = f32[3,2,16,1024]{3,2,1,0:T(8,128)S(1)} collective-permute-done((f32[3,2,16,1024]{3,2,1,0:T(8,128)S(1)}, f32[3,2,16,1024]{3,2,1,0:T(8,128)S(1)}, u32[]{:S(2)}, u32[]{:S(2)}) %collective-permute-start.1) | collective-permute-done | bytes 393248 | tf_op jit(solution)/shard_map/ppermute | solution.py:243
  19.4 0.1 broadcast_in_dim.10.tab_ref
  19.4 0.0 copy-start.1
  19.5 2.8 %copy-done.1 = f32[3,32,16,1024]{3,2,1,0:T(8,128)S(1)} copy-done((f32[3,32,16,1024]{3,2,1,0:T(8,128)S(1)}, f32[3,32,16,1024]{3,2,1,0:T(8,128)}, u32[]{:S(2)}) %copy-start.1) | copy-done | bytes 6291480
  22.2 12.0 %main_pass.1 = (f32[4,16,1024]{2,1,0:T(8,128)S(1)}, f32[4,2,8,8,1024]{4,3,2,1,0:T(8,128)S(1)}) custom-call(f32[3,32,16,1024]{3,2,1,0:T(8,128)S(1)} %copy-done.1, f32[3,2,16,1024]{3,2,1,0:T(8,128)S(1)} %collective-permute-done.zlo_hbm, f32[3,2,16,1024]{3,2,1,0:T(8,128)S(1)} %collective-permute-done.1.zhi_hbm, f32[16,8,128]{2,1,0:T(8,128)S(1)} %broadcast_in_dim.10.tab_ref), custom_call_target="tpu_custom_call" | custom-call | flops 60000000 | bytes 10000000 | tf_op jit(solution)/shard_map/main_pass/pallas_call | solution.py:154
  34.3 0.0 collective-permute-done.2.lo_ref
  34.3 0.0 collective-permute-done.3.hi_ref
  34.3 1.2 %edge_pass.1 = f32[8,4,16,128]{3,2,1,0:T(8,128)S(1)} custom-call(f32[4,2,8,8,1024]{4,3,2,1,0:T(8,128)S(1)} %get-tuple-element.13.edge_ref, f32[3,8,8,1024]{3,2,1,0:T(8,128)S(1)} %collective-permute-done.2.lo_ref, f32[3,8,8,1024]{3,2,1,0:T(8,128)S(1)} %collective-permute-done.3.hi_ref, f32[4,16,1024]{2,1,0:T(8,128)S(1)} %get-tuple-element.16.comp_ref, ...), custom_call_target="tpu_custom_call" | custom-call | flops 10000000 | bytes 4000000 | tf_op jit(solution)/shard_map/edge_pass/pallas_call | solution.py:198
  35.6 17.5 %all_to_all.5.parts_ref = f32[8,4,16,128]{3,2,1,0:T(8,128)} all-to-all(f32[8,4,16,128]{3,2,1,0:T(8,128)S(1)} %edge_pass.1), channel_id=1, replica_groups=mesh['depth'=8,'tile'=16] {'depth'}, dimensions={0} | all-to-all | bytes 524288 | tf_op jit(solution)/shard_map/all_to_all | solution.py:246
  53.0 1.6 %over.1 = f32[4,16,128]{2,1,0:T(8,128)} custom-call(f32[8,4,16,128]{3,2,1,0:T(8,128)} %all_to_all.5.parts_ref), custom_call_target="tpu_custom_call" | custom-call | tf_op jit(solution)/shard_map/over/pallas_call | solution.py:220
  (3 shorter events, 0.0 us)
Async XLA Ops:
  0.0 2.8 %copy-start = (f32[3,32,16,1024]{3,2,1,0:T(8,128)S(1)}, f32[3,32,16,1024]{3,2,1,0:T(8,128)}, u32[]{:S(2)}) copy-start(f32[3,32,16,1024]{3,2,1,0:T(8,128)} %v_hbm.1) | copy-start | bytes 18874372
  2.8 12.5 %copy-start.3 = (f32[16]{0:T(128)S(1)}, f32[16]{0:T(128)}, u32[]{:S(2)}) copy-start(f32[16]{0:T(128)} %param.4) | copy-start | bytes 196
  2.8 12.5 %copy-start.2 = (f32[3,16]{1,0:T(4,128)S(1)}, f32[3,16]{1,0:T(4,128)}, u32[]{:S(2)}) copy-start(f32[3,16]{1,0:T(4,128)} %param.5) | copy-start | bytes 580
  4.7 29.6 %collective-permute-start.2 = (f32[3,8,8,1024]{3,2,1,0:T(8,128)}, f32[3,8,8,1024]{3,2,1,0:T(8,128)S(1)}, u32[]{:S(2)}, u32[]{:S(2)}) collective-permute-start(f32[3,8,8,1024]{3,2,1,0:T(8,128)} %get-tuple-element.14), channel_id=1, source_target_pairs={{0,1},{1,2},{2,3},{3,4},{4,5},{5,6},{6,7},{7,8},{8,9},{9,10},{10,1... | collective-permute-start | bytes 2359304 | tf_op jit(solution)/shard_map/ppermute | solution.py:240
  8.1 26.2 %collective-permute-start.3 = (f32[3,8,8,1024]{3,2,1,0:T(8,128)S(1)}, f32[3,8,8,1024]{3,2,1,0:T(8,128)S(1)}, u32[]{:S(2)}, u32[]{:S(2)}) collective-permute-start(f32[3,8,8,1024]{3,2,1,0:T(8,128)S(1)} %get-tuple-element.15), channel_id=1, source_target_pairs={{1,0},{2,1},{3,2},{4,3},{5,4},{6,5},{7,6},{8,7},{9,8},{10,9},{11,1... | collective-permute-start | bytes 2359304 | tf_op jit(solution)/shard_map/ppermute | solution.py:241
  12.6 2.8 %collective-permute-start = (f32[3,2,16,1024]{3,2,1,0:T(8,128)}, f32[3,2,16,1024]{3,2,1,0:T(8,128)S(1)}, u32[]{:S(2)}, u32[]{:S(2)}) collective-permute-start(f32[3,2,16,1024]{3,2,1,0:T(8,128)} %get-tuple-element.11), channel_id=1, source_target_pairs={{0,16},{16,32},{32,48},{48,64},{64,80},{80,96},{96,112},{1,17},{17... | collective-permute-start | bytes 1179656 | tf_op jit(solution)/shard_map/ppermute | solution.py:242
  14.0 5.4 %collective-permute-start.1 = (f32[3,2,16,1024]{3,2,1,0:T(8,128)S(1)}, f32[3,2,16,1024]{3,2,1,0:T(8,128)S(1)}, u32[]{:S(2)}, u32[]{:S(2)}) collective-permute-start(f32[3,2,16,1024]{3,2,1,0:T(8,128)S(1)} %get-tuple-element.12), channel_id=1, source_target_pairs={{16,0},{32,16},{48,32},{64,48},{80,64},{96,80},{112,96},{17,1},{33... | collective-permute-start | bytes 1179656 | tf_op jit(solution)/shard_map/ppermute | solution.py:243
  19.4 2.8 %copy-start.1 = (f32[3,32,16,1024]{3,2,1,0:T(8,128)S(1)}, f32[3,32,16,1024]{3,2,1,0:T(8,128)}, u32[]{:S(2)}) copy-start(f32[3,32,16,1024]{3,2,1,0:T(8,128)} %v_hbm.1) | copy-start | bytes 18874372

commit v2 on v1

v2 whole, which is shorter than its diff:
```python
import jax
import jax.numpy as jnp
from jax import lax
from jax.experimental import pallas as pl
from jax.experimental.pallas import tpu as pltpu
from jax.sharding import PartitionSpec as P

F32 = jnp.float32
VMEM_LIMIT = 40 * 1024 * 1024
VMEM_ALL = 50 * 1024 * 1024
QSCALE = -1.0 / 1152.0


def shift_up(count):
    return [(i, i + 1) for i in range(count - 1)]


def shift_down(count):
    return [(i + 1, i) for i in range(count - 1)]


def pack_kernel(v_ref, up_ref, down_ref, zup_ref, zdown_ref):
    half = pl.program_id(1)

    @pl.when(half == 0)
    def _():
        zdown_ref[...] = v_ref[:, 0, 0:2]

    @pl.when(half == 1)
    def _():
        zup_ref[...] = v_ref[:, 3, 2:4]

    row = lax.broadcasted_iota(jnp.int32, (8, 1024), 0)
    for quarter in range(4):
        for zz in range(4):
            low = v_ref[0, quarter, zz, 0:8, :]
            high = v_ref[0, quarter, zz, 8:16, :]
            up = jnp.where(row == 6, high - 8.0 * pltpu.roll(high, 7, 0), high)
            down = jnp.where(row == 0, -low, 8.0 * pltpu.roll(low, 1, 0) - low)
            up_ref[0, zz, 2 * quarter : 2 * quarter + 2, :] = up[6:8]
            down_ref[0, zz, 2 * quarter : 2 * quarter + 2, :] = down[0:2]


def pack(velocity):
    comps, depth, width, length = velocity.shape
    ends = jax.ShapeDtypeStruct((comps, 8, 8, length), F32)
    layers = jax.ShapeDtypeStruct((comps, 2, width, length), F32)
    end_block = pl.BlockSpec((1, 4, 8, length), lambda c, h: (c, h, 0, 0))
    layer_block = pl.BlockSpec((1, 2, width, length), lambda c, h: (c, 0, 0, 0))
    return pl.pallas_call(
        pack_kernel,
        grid=(comps, 2),
        in_specs=[pl.BlockSpec((1, 4, 4, width, length), lambda c, h: (c, 0, h, 0, 0))],
        out_specs=[end_block] * 2 + [layer_block] * 2,
        out_shape=[ends, ends, layers, layers],
        compiler_params=pltpu.CompilerParams(vmem_limit_bytes=VMEM_ALL),
        cost_estimate=pl.CostEstimate(flops=2000000, bytes_accessed=9000000, transcendentals=0),
        name="pack",
    )(velocity.reshape(comps, 4, 8, width, length))


def lookup(qcrit, tab_ref):
    pos = 7.5 * jnp.tanh(qcrit) + 7.5
    index = jnp.minimum(pos.astype(jnp.int32), 14)
    low, index = index < 8, index & 7
    pick = lambda k: jnp.take_along_axis(tab_ref[k], index, axis=0, mode="promise_in_bounds")
    base = [jnp.where(low, pick(2 * k), pick(2 * k + 1)) for k in range(8)]
    vals = [base[k] + base[k + 4] * pos for k in range(4)]
    return jnp.exp(vals[0]), vals[1:]


def composite(carry, step, colors):
    trans, shades = carry
    after = trans * step
    weight = trans - after
    return after, [s + weight * c for s, c in zip(shades, colors)]


def edge_masks():
    row = lax.broadcasted_iota(jnp.int32, (8, 128), 0)
    lane = lax.broadcasted_iota(jnp.int32, (8, 128), 1)
    return (row < 1, row > 6, row < 2, row > 5), (lane < 1, lane > 126, lane < 2, lane > 125)


def gradients(window, others, lefts, rights, side, masks):
    (r1, r7, r2, r6), (l1, l7, l2, l6) = masks
    dz, dx, dy = [], [], []
    for c in range(3):
        w = window[c]
        center = w[2]
        dz.append(8.0 * (w[3] - w[1]) - (w[4] - w[0]))
        above, below = (0.0, others[c]) if side == 0 else (others[c], 0.0)
        p1 = pltpu.roll(jnp.where(r1, below, center), 7, 0)
        m1 = pltpu.roll(jnp.where(r7, above, center), 1, 0)
        p2 = pltpu.roll(jnp.where(r2, below, center), 6, 0)
        m2 = pltpu.roll(jnp.where(r6, above, center), 2, 0)
        dx.append(8.0 * (p1 - m1) - (p2 - m2))
        p1 = pltpu.roll(jnp.where(l1, rights[c], center), 127, 1)
        m1 = pltpu.roll(jnp.where(l7, lefts[c], center), 1, 1)
        p2 = pltpu.roll(jnp.where(l2, rights[c], center), 126, 1)
        m2 = pltpu.roll(jnp.where(l6, lefts[c], center), 2, 1)
        dy.append(8.0 * (p1 - m1) - (p2 - m2))
    return dz, dx, dy


def invariant(dz, dx, dy):
    cross = dz[1] * dx[0] + dz[2] * dy[0] + dx[2] * dy[1]
    return dz[0] * dz[0] + dx[1] * dx[1] + dy[2] * dy[2] + 2.0 * cross


def edge_terms(total, dz, dx, dy):
    return total, 2.0 * dz[1], 2.0 * dx[1], 2.0 * dy[1]


def middle_kernel(v_hbm, tab_ref, comp_ref, edge_ref, buf, sems):
    j = pl.program_id(0)

    def copy(k):
        lanes = pl.ds(pl.multiple_of(k * 128, 128), 128)
        inner = pl.ds(pl.multiple_of((k + 1) * 128, 128), 128)
        return pltpu.make_async_copy(v_hbm.at[:, :, :, lanes], buf.at[:, :, :, inner], sems.at[k])

    @pl.when(j == 0)
    def _():
        for k in range(8):
            copy(k).start()
        zeros = jnp.zeros((3, 32, 16, 128), F32)
        buf[:, :, :, 0:128] = zeros
        buf[:, :, :, 9 * 128 : 10 * 128] = zeros
        copy(0).wait()

    @pl.when(j < 7)
    def _():
        copy(j + 1).wait()

    masks = edge_masks()
    left = pl.ds(pl.multiple_of(j * 128, 128), 128)
    mid = pl.ds(pl.multiple_of(j * 128 + 128, 128), 128)
    right = pl.ds(pl.multiple_of(j * 128 + 256, 128), 128)
    for side in range(2):
        rows = slice(8 * side, 8 * side + 8)
        others = slice(8 - 8 * side, 16 - 8 * side)
        zeros = jnp.zeros((8, 128), F32)
        carry = (zeros + 1.0, [zeros] * 3)
        lines = [[buf[c, z, rows, mid] for z in range(32)] for c in range(3)]
        for z in range(2, 30):
            quarter, zz = z // 8, z % 8
            dz, dx, dy = gradients(
                [lines[c][z - 2 : z + 3] for c in range(3)],
                [buf[c, z, others, mid] for c in range(3)],
                [buf[c, z, rows, left] for c in range(3)],
                [buf[c, z, rows, right] for c in range(3)],
                side,
                masks,
            )
            total = invariant(dz, dx, dy)
            ends = slice(6 * side, 6 * side + 2)
            for e, value in enumerate(edge_terms(total, dz, dx, dy)):
                edge_ref[e, side, zz, 2 * quarter : 2 * quarter + 2, :] = value[ends]
            step, colors = lookup(QSCALE * total, tab_ref)
            carry = composite(carry, step, colors)
        for c in range(3):
            comp_ref[c, rows, :] = carry[1][c]
        comp_ref[3, rows, :] = carry[0]


def middle_pass(velocity, table):
    comps, depth, width, length = velocity.shape
    return pl.pallas_call(
        middle_kernel,
        grid=(8,),
        in_specs=[pl.BlockSpec(memory_space=pl.ANY), pl.BlockSpec((16, 8, 128), lambda j: (0, 0, 0))],
        out_specs=[
            pl.BlockSpec((4, width, 128), lambda j: (0, 0, j)),
            pl.BlockSpec((4, 2, 8, 8, 128), lambda j: (0, 0, 0, 0, j)),
        ],
        out_shape=[
            jax.ShapeDtypeStruct((4, width, length), F32),
            jax.ShapeDtypeStruct((4, 2, 8, 8, length), F32),
        ],
        scratch_shapes=[pltpu.VMEM((comps, depth, width, length + 256), F32), pltpu.SemaphoreType.DMA((8,))],
        compiler_params=pltpu.CompilerParams(vmem_limit_bytes=VMEM_ALL),
        cost_estimate=pl.CostEstimate(flops=60000000, bytes_accessed=10000000, transcendentals=1000000),
        name="middle_pass",
    )(velocity, table)


def ends_kernel(v_hbm, zlo_ref, zhi_ref, comp_ref, tab_ref, out_ref, edge_ref, buf, sems):
    copies = [pltpu.make_async_copy(v_hbm.at[:, 28 * k : 28 * k + 4], buf.at[k], sems.at[k]) for k in range(2)]
    for copy in copies:
        copy.start()
    for copy in copies:
        copy.wait()
    masks = edge_masks()
    zeros = jnp.zeros((8, 128), F32)
    for j in range(8):
        lanes = slice(j * 128, j * 128 + 128)
        for side in range(2):
            rows = slice(8 * side, 8 * side + 8)
            others = slice(8 - 8 * side, 16 - 8 * side)
            carry = (zeros + 1.0, [zeros] * 3)
            for k in range(2):
                first = [[zlo_ref[c, i, rows, lanes] for i in range(2)] for c in range(3)] if k == 0 else [[]] * 3
                last = [[zhi_ref[c, i, rows, lanes] for i in range(2)] for c in range(3)] if k == 1 else [[]] * 3
                lines = [first[c] + [buf[k, c, i, rows, lanes] for i in range(4)] + last[c] for c in range(3)]
                for i in range(2):
                    at = i + 2 * k
                    sideways = lambda m: [
                        buf[k, c, at, rows, m * 128 : m * 128 + 128] if 0 <= m < 8 else zeros for c in range(3)
                    ]
                    dz, dx, dy = gradients(
                        [lines[c][i : i + 5] for c in range(3)],
                        [buf[k, c, at, others, lanes] for c in range(3)],
                        sideways(j - 1),
                        sideways(j + 1),
                        side,
                        masks,
                    )
                    total = invariant(dz, dx, dy)
                    ends = slice(6 * side, 6 * side + 2)
                    for e, value in enumerate(edge_terms(total, dz, dx, dy)):
                        edge_ref[e, side, i, 6 * k : 6 * k + 2, lanes] = value[ends]
                    step, colors = lookup(QSCALE * total, tab_ref)
                    carry = composite(carry, step, colors)
                if k == 0:
                    trans, shades = carry
                    shades = [s + trans * comp_ref[c, rows, lanes] for c, s in enumerate(shades)]
                    carry = (trans * comp_ref[3, rows, lanes], shades)
            for c in range(3):
                out_ref[c, rows, lanes] = carry[1][c]
            out_ref[3, rows, lanes] = carry[0]


def ends_pass(velocity, before, after, comp, table):
    comps, depth, width, length = velocity.shape
    vmem = pl.BlockSpec(memory_space=pltpu.VMEM)
    return pl.pallas_call(
        ends_kernel,
        in_specs=[pl.BlockSpec(memory_space=pl.ANY)] + [vmem] * 4,
        out_shape=[
            jax.ShapeDtypeStruct((4, width, length), F32),
            jax.ShapeDtypeStruct((4, 2, 2, 8, length), F32),
        ],
        scratch_shapes=[pltpu.VMEM((2, comps, 4, width, length), F32), pltpu.SemaphoreType.DMA((2,))],
        compiler_params=pltpu.CompilerParams(vmem_limit_bytes=VMEM_ALL),
        cost_estimate=pl.CostEstimate(flops=8000000, bytes_accessed=3000000, transcendentals=130000),
        name="ends_pass",
    )(velocity, before, after, comp, table)


def edge_kernel(edge_ref, ends_ref, lo_ref, hi_ref, comp_ref, tab_ref, out_ref):
    row = lax.broadcasted_iota(jnp.int32, (8, 128), 0)
    first, last = row < 2, row > 5
    for j in range(8):
        lanes = slice(j * 128, j * 128 + 128)
        out_ref[j] = comp_ref[:, :, lanes]
        for side, halo_ref in enumerate((lo_ref, hi_ref)):
            zeros = jnp.zeros((8, 128), F32)
            carry = (zeros + 1.0, [zeros] * 3)
            for zz in range(8):
                terms = [edge_ref[e, side, zz, :, lanes] for e in range(4)]
                if zz < 2:
                    terms = [jnp.where(first, ends_ref[e, side, zz, :, lanes], t) for e, t in enumerate(terms)]
                if zz > 5:
                    terms = [jnp.where(last, ends_ref[e, side, zz - 6, :, lanes], t) for e, t in enumerate(terms)]
                part, by_z, by_x, by_y = terms
                hz, hx, hy = [halo_ref[c, zz, :, lanes] for c in range(3)]
                total = part + by_z * hz + by_y * hy + hx * (by_x + hx)
                step, colors = lookup(QSCALE * total, tab_ref)
                carry = composite(carry, step, colors)
            trans, shades = carry
            for back in (2, 4):
                shades = [s + trans * pltpu.roll(s, 8 - back, 0) for s in shades]
                trans = trans * pltpu.roll(trans, 8 - back, 0)
            start = 14 * side
            for c in range(3):
                out_ref[j, c, start : start + 2, :] = shades[c][0:2]
            out_ref[j, 3, start : start + 2, :] = trans[0:2]


def edge_pass(edge, ends, lo, hi, comp, table):
    width = comp.shape[1]
    return pl.pallas_call(
        edge_kernel,
        out_shape=jax.ShapeDtypeStruct((8, 4, width, 128), F32),
        compiler_params=pltpu.CompilerParams(vmem_limit_bytes=VMEM_LIMIT),
        cost_estimate=pl.CostEstimate(flops=10000000, bytes_accessed=4000000, transcendentals=300000),
        name="edge_pass",
    )(edge, ends, lo, hi, comp, table)


def over(parts):
    result = parts[7]
    for layer in range(6, -1, -1):
        front = parts[layer]
        shade = front[:3] + front[3:] * result[:3]
        result = jnp.concatenate([shade, front[3:] * result[3:]], axis=0)
    return result


def make_table(sigma_table, color_table, depth_total):
    values = jnp.concatenate([sigma_table[None] * (-1.0 / depth_total), color_table], axis=0)
    slopes = values[:, 1:] - values[:, :-1]
    starts = values[:, :-1] - slopes * jnp.arange(15, dtype=F32)
    table = jnp.concatenate([starts, slopes], axis=0)
    table = jnp.pad(table, ((0, 0), (0, 1))).reshape(16, 8, 1)
    return jnp.broadcast_to(table, (16, 8, 128))


def local(velocity, sigma_table, color_table):
    layers, tiles = lax.axis_size("depth"), lax.axis_size("tile")
    table = make_table(sigma_table, color_table, velocity.shape[1] * layers)
    up, down, zup, zdown = pack(velocity)
    lo = lax.ppermute(up, "tile", shift_up(tiles))
    hi = lax.ppermute(down, "tile", shift_down(tiles))
    before = lax.ppermute(zup, "depth", shift_up(layers))
    after = lax.ppermute(zdown, "depth", shift_down(layers))
    comp, edge = middle_pass(velocity, table)
    comp, ends = ends_pass(velocity, before, after, comp, table)
    pieces = edge_pass(edge, ends, lo, hi, comp, table)
    received = lax.all_to_all(pieces, "depth", split_axis=0, concat_axis=0, tiled=True)
    return over(received)


def solution(mesh):
    return jax.shard_map(
        local,
        mesh=mesh,
        in_specs=(P(None, "depth", "tile", None), P(), P()),
        out_specs=P(None, "tile", "depth"),
        check_vma=False,
    )
```

time: 54.9 us -> 47.3 us (0.86)
  local copies, waits for them, and re-layouts: 5.73 us -> 0.16 us
  waiting for transfers between devices: 3.9 us -> 0.01 us
  Pallas kernels: 16.8 us -> 20.6 us
  blocking collectives: 17.5 us -> 14.8 us
  other arithmetic: 0.1 us -> 0.76 us
    unnamed x8 -> x4, local copies, waits for them, and re-layouts: 5.58 us -> 0.01 us
    ppermute x1, waiting for transfers between devices: 3.89 us -> 0.01 us  [local(): after = lax.ppermute(zdown, 'depth', shift_down(layers))]
    pallas_call x3, Pallas kernels: 15.5 us -> 19.2 us  [the longest x1 10.9 us: middle_pass(): pl.pallas_call(middle_kernel, grid=(8,), in_specs=[pl.BlockSpec(memory_sp...]
    all_to_all x1, blocking collectives: 17.5 us -> 14.8 us  [local(): lax.all_to_all(pieces, 'depth', split_axis=0, concat_axis=0, tiled=True)]
    concatenate x0 -> x1, other arithmetic: none -> 0.62 us  [over(): result = jnp.concatenate([shade, front[3:] * result[3:]], axis=0)]
  transfers between devices with their start and end apart: 4 -> 4, of which waited for: 1 -> 0; matrix products, arithmetic and copies ran while one was open for 0% -> 1% of each run, Pallas kernels for 22% -> 29%
where the time goes in v2:
time: 47.3 us; the launch traced here: 46.9 us
  Pallas kernels  20.6 us (44%)
  blocking collectives  14.8 us (31%)
  starting transfers between devices  10.5 us (22%)
  other arithmetic  0.76 us (2%)
    all_to_all x1, blocking collectives, local(): lax.all_to_all(pieces, 'depth', split_axis=0, concat_axis=0, tiled=True)  14.8 us
    pallas_call x1, Pallas kernels, middle_pass(): pl.pallas_call(middle_kernel, grid=(8,), in_specs=[pl.BlockSpec(memory_sp...  10.9 us
    pallas_call x1, Pallas kernels, pack(): pl.pallas_call(pack_kernel, grid=(comps, 2), in_specs=[pl.BlockSpec((1, 4...  5.63 us
    ppermute x1, starting transfers between devices, local(): hi = lax.ppermute(down, 'tile', shift_down(tiles))  4.55 us
    ppermute x1, starting transfers between devices, local(): lo = lax.ppermute(up, 'tile', shift_up(tiles))  3.39 us
    pallas_call x1, Pallas kernels, ends_pass(): pl.pallas_call(ends_kernel, in_specs=[pl.BlockSpec(memory_space=pl.ANY)]...  2.67 us
    pallas_call x1, Pallas kernels, edge_pass(): pl.pallas_call(edge_kernel, out_shape=jax.ShapeDtypeStruct((8, 4, width,...  1.32 us
    ppermute x1, starting transfers between devices, local(): before = lax.ppermute(zup, 'depth', shift_up(layers))  1.31 us
  transfers between devices with their start and end apart: 4, of which 0 were waited for; matrix products, arithmetic and copies ran while one was open for 1% of the time, Pallas kernels for 29%

profile of v2, /device:TPU:32, one launch (start us, length us, event | category | flops | bytes accessed | tf_op | source)
XLA Modules:
  0.0 46.9 jit_solution(2703065182585292474)
XLA Ops:
  0.0 0.0 copy-start.1
  0.0 0.0 copy-start
  0.0 5.6 %pack.1 = (f32[3,8,8,1024]{3,2,1,0:T(8,128)}, f32[3,8,8,1024]{3,2,1,0:T(8,128)S(1)}, f32[3,2,16,1024]{3,2,1,0:T(8,128)}, f32[3,2,16,1024]{3,2,1,0:T(8,128)S(1)}) custom-call(f32[3,4,8,16,1024]{4,3,2,1,0:T(8,128)} %bitcast.77), custom_call_target="tpu_custom_call" | custom-call | flops 2000000 | bytes 9000000 | tf_op jit(solution)/shard_map/pack/pallas_call | solution.py:50
  5.6 3.4 %collective-permute-start.2 = (f32[3,8,8,1024]{3,2,1,0:T(8,128)}, f32[3,8,8,1024]{3,2,1,0:T(8,128)S(1)}, u32[]{:S(2)}, u32[]{:S(2)}) collective-permute-start(f32[3,8,8,1024]{3,2,1,0:T(8,128)} %get-tuple-element.18), channel_id=1, source_target_pairs={{0,1},{1,2},{2,3},{3,4},{4,5},{5,6},{6,7},{7,8},{8,9},{9,10},{10,1... | collective-permute-start | bytes 2359304 | tf_op jit(solution)/shard_map/ppermute | solution.py:314
  9.0 4.6 %collective-permute-start.3 = (f32[3,8,8,1024]{3,2,1,0:T(8,128)S(1)}, f32[3,8,8,1024]{3,2,1,0:T(8,128)S(1)}, u32[]{:S(2)}, u32[]{:S(2)}) collective-permute-start(f32[3,8,8,1024]{3,2,1,0:T(8,128)S(1)} %get-tuple-element.19), channel_id=1, source_target_pairs={{1,0},{2,1},{3,2},{4,3},{5,4},{6,5},{7,6},{8,7},{9,8},{10,9},{11,1... | collective-permute-start | bytes 2359304 | tf_op jit(solution)/shard_map/ppermute | solution.py:315
  13.6 1.3 %collective-permute-start = (f32[3,2,16,1024]{3,2,1,0:T(8,128)}, f32[3,2,16,1024]{3,2,1,0:T(8,128)S(1)}, u32[]{:S(2)}, u32[]{:S(2)}) collective-permute-start(f32[3,2,16,1024]{3,2,1,0:T(8,128)} %get-tuple-element.14), channel_id=1, source_target_pairs={{0,16},{16,32},{32,48},{48,64},{64,80},{80,96},{96,112},{1,17},{17... | collective-permute-start | bytes 1179656 | tf_op jit(solution)/shard_map/ppermute | solution.py:316
  14.9 1.3 %collective-permute-start.1 = (f32[3,2,16,1024]{3,2,1,0:T(8,128)S(1)}, f32[3,2,16,1024]{3,2,1,0:T(8,128)S(1)}, u32[]{:S(2)}, u32[]{:S(2)}) collective-permute-start(f32[3,2,16,1024]{3,2,1,0:T(8,128)S(1)} %get-tuple-element.15), channel_id=1, source_target_pairs={{16,0},{32,16},{48,32},{64,48},{80,64},{96,80},{112,96},{17,1},{33... | collective-permute-start | bytes 1179656 | tf_op jit(solution)/shard_map/ppermute | solution.py:317
  16.2 0.0 copy-done.1
  16.2 0.0 copy-done
  16.3 0.1 multiply_subtract_fusion
  16.3 0.1 broadcast_in_dim.4
  16.4 0.1 broadcast_in_dim.10.tab_ref
  16.5 10.9 %middle_pass.1 = (f32[4,16,1024]{2,1,0:T(8,128)S(1)}, f32[4,2,8,8,1024]{4,3,2,1,0:T(8,128)S(1)}) custom-call(f32[3,32,16,1024]{3,2,1,0:T(8,128)} %v_hbm.3, f32[16,8,128]{2,1,0:T(8,128)S(1)} %broadcast_in_dim.10.tab_ref), custom_call_target="tpu_custom_call" | custom-call | flops 60000000 | bytes 10000000 | tf_op jit(solution)/shard_map/middle_pass/pallas_call | solution.py:169
  27.5 0.0 collective-permute-done.zlo_ref
  27.5 0.0 collective-permute-done.1.zhi_ref
  27.5 2.7 %ends_pass.1 = (f32[4,16,1024]{2,1,0:T(8,128)S(1)}, f32[4,2,2,8,1024]{4,3,2,1,0:T(8,128)S(1)}) custom-call(f32[3,32,16,1024]{3,2,1,0:T(8,128)} %v_hbm.3, f32[3,2,16,1024]{3,2,1,0:T(8,128)S(1)} %collective-permute-done.zlo_ref, f32[3,2,16,1024]{3,2,1,0:T(8,128)S(1)} %collective-permute-done.1.zhi_ref, f32[4,16,1024]{2,1,0:T(8,128)S(1)} %get-tuple-element.16.comp_ref, ...), custom_call_target="tpu_custom_call" | custom-call | flops 8000000 | bytes 3000000 | tf_op jit(solution)/shard_map/ends_pass/pallas_call | solution.py:237
  30.2 0.0 collective-permute-done.2.lo_ref
  30.2 0.0 collective-permute-done.3.hi_ref
  30.2 1.3 %edge_pass.1 = f32[8,4,16,128]{3,2,1,0:T(8,128)S(1)} custom-call(f32[4,2,8,8,1024]{4,3,2,1,0:T(8,128)S(1)} %get-tuple-element.13.edge_ref, f32[4,2,2,8,1024]{4,3,2,1,0:T(8,128)S(1)} %get-tuple-element.17.ends_ref, f32[3,8,8,1024]{3,2,1,0:T(8,128)S(1)} %collective-permute-done.2.lo_ref, f32[3,8,8,1024]{3,2,1,0:T(8,128)S(1)} %collective-permute-done.3.hi_ref, ...), custom_call_target="tpu_custom_call" | custom-call | flops 10000000 | bytes 4000000 | tf_op jit(solution)/shard_map/edge_pass/pallas_call | solution.py:283
  31.5 14.8 %all_to_all.5 = f32[8,4,16,128]{3,2,1,0:T(8,128)S(1)} all-to-all(f32[8,4,16,128]{3,2,1,0:T(8,128)S(1)} %edge_pass.1), channel_id=1, replica_groups=mesh['depth'=8,'tile'=16] {'depth'}, dimensions={0} | all-to-all | bytes 524288 | tf_op jit(solution)/shard_map/all_to_all | solution.py:321
  46.3 0.6 %pad_maximum_fusion = f32[4,16,128]{2,1,0:T(8,128)} fusion(f32[1,16,128]{2,1,0:T(8,128)S(1)} %get-tuple-element.26, f32[3,16,128]{2,1,0:T(8,128)S(1)} %fusion.13), kind=kLoop, calls=%fused_computation | loop fusion | flops 8192 | bytes 65536 | tf_op jit(solution)/shard_map/concatenate | solution.py:297
  (5 shorter events, 0.1 us)
Async XLA Ops:
  0.0 16.2 %copy-start.1 = (f32[16]{0:T(128)S(1)}, f32[16]{0:T(128)}, u32[]{:S(2)}) copy-start(f32[16]{0:T(128)} %param.4) | copy-start | bytes 196
  0.0 16.2 %copy-start = (f32[3,16]{1,0:T(4,128)S(1)}, f32[3,16]{1,0:T(4,128)}, u32[]{:S(2)}) copy-start(f32[3,16]{1,0:T(4,128)} %param.5) | copy-start | bytes 580
  5.6 24.5 %collective-permute-start.2 = (f32[3,8,8,1024]{3,2,1,0:T(8,128)}, f32[3,8,8,1024]{3,2,1,0:T(8,128)S(1)}, u32[]{:S(2)}, u32[]{:S(2)}) collective-permute-start(f32[3,8,8,1024]{3,2,1,0:T(8,128)} %get-tuple-element.18), channel_id=1, source_target_pairs={{0,1},{1,2},{2,3},{3,4},{4,5},{5,6},{6,7},{7,8},{8,9},{9,10},{10,1... | collective-permute-start | bytes 2359304 | tf_op jit(solution)/shard_map/ppermute | solution.py:314
  9.0 21.1 %collective-permute-start.3 = (f32[3,8,8,1024]{3,2,1,0:T(8,128)S(1)}, f32[3,8,8,1024]{3,2,1,0:T(8,128)S(1)}, u32[]{:S(2)}, u32[]{:S(2)}) collective-permute-start(f32[3,8,8,1024]{3,2,1,0:T(8,128)S(1)} %get-tuple-element.19), channel_id=1, source_target_pairs={{1,0},{2,1},{3,2},{4,3},{5,4},{6,5},{7,6},{8,7},{9,8},{10,9},{11,1... | collective-permute-start | bytes 2359304 | tf_op jit(solution)/shard_map/ppermute | solution.py:315
  13.6 13.9 %collective-permute-start = (f32[3,2,16,1024]{3,2,1,0:T(8,128)}, f32[3,2,16,1024]{3,2,1,0:T(8,128)S(1)}, u32[]{:S(2)}, u32[]{:S(2)}) collective-permute-start(f32[3,2,16,1024]{3,2,1,0:T(8,128)} %get-tuple-element.14), channel_id=1, source_target_pairs={{0,16},{16,32},{32,48},{48,64},{64,80},{80,96},{96,112},{1,17},{17... | collective-permute-start | bytes 1179656 | tf_op jit(solution)/shard_map/ppermute | solution.py:316
  14.9 12.6 %collective-permute-start.1 = (f32[3,2,16,1024]{3,2,1,0:T(8,128)S(1)}, f32[3,2,16,1024]{3,2,1,0:T(8,128)S(1)}, u32[]{:S(2)}, u32[]{:S(2)}) collective-permute-start(f32[3,2,16,1024]{3,2,1,0:T(8,128)S(1)} %get-tuple-element.15), channel_id=1, source_target_pairs={{16,0},{32,16},{48,32},{64,48},{80,64},{96,80},{112,96},{17,1},{33... | collective-permute-start | bytes 1179656 | tf_op jit(solution)/shard_map/ppermute | solution.py:317

commit v3 on v2

--- a/solution.py
+++ b/solution.py
@@ -11,52 +11,53 @@
 QSCALE = -1.0 / 1152.0
 
 
-def shift_up(count):
-    return [(i, i + 1) for i in range(count - 1)]
-
-
-def shift_down(count):
-    return [(i + 1, i) for i in range(count - 1)]
-
-
-def pack_kernel(v_ref, up_ref, down_ref, zup_ref, zdown_ref):
-    half = pl.program_id(1)
-
-    @pl.when(half == 0)
-    def _():
-        zdown_ref[...] = v_ref[:, 0, 0:2]
-
-    @pl.when(half == 1)
-    def _():
-        zup_ref[...] = v_ref[:, 3, 2:4]
-
+def ring(count, by):
+    return [(i, (i + by) % count) for i in range(count)]
+
+
+def pack_kernel(v_hbm, up_ref, down_ref, zup_ref, zdown_ref, buf, sems):
+    copies = [
+        [pltpu.make_async_copy(v_hbm.at[c, 8 * q : 8 * q + 8], buf.at[c, 8 * q : 8 * q + 8], sems.at[c, q]) for q in range(4)]
+        for c in range(3)
+    ]
+    for some in copies:
+        for copy in some:
+            copy.start()
+    tile, tiles = lax.axis_index("tile"), lax.axis_size("tile")
+    layer, layers = lax.axis_index("depth"), lax.axis_size("depth")
+    keep_up = jnp.where(tile == tiles - 1, 0.0, 1.0)
+    keep_down = jnp.where(tile == 0, 0.0, 1.0)
+    keep_zup = jnp.where(layer == layers - 1, 0.0, 1.0)
+    keep_zdown = jnp.where(layer == 0, 0.0, 1.0)
     row = lax.broadcasted_iota(jnp.int32, (8, 1024), 0)
-    for quarter in range(4):
-        for zz in range(4):
-            low = v_ref[0, quarter, zz, 0:8, :]
-            high = v_ref[0, quarter, zz, 8:16, :]
-            up = jnp.where(row == 6, high - 8.0 * pltpu.roll(high, 7, 0), high)
-            down = jnp.where(row == 0, -low, 8.0 * pltpu.roll(low, 1, 0) - low)
-            up_ref[0, zz, 2 * quarter : 2 * quarter + 2, :] = up[6:8]
-            down_ref[0, zz, 2 * quarter : 2 * quarter + 2, :] = down[0:2]
+    for c in range(3):
+        for quarter in range(4):
+            copies[c][quarter].wait()
+            for zz in range(8):
+                z = quarter * 8 + zz
+                low = buf[c, z, 0:8, :]
+                high = buf[c, z, 8:16, :]
+                up = jnp.where(row == 6, high - 8.0 * pltpu.roll(high, 7, 0), high)
+                down = jnp.where(row == 0, -low, 8.0 * pltpu.roll(low, 1, 0) - low)
+                up_ref[c, zz, 2 * quarter : 2 * quarter + 2, :] = keep_up * up[6:8]
+                down_ref[c, zz, 2 * quarter : 2 * quarter + 2, :] = keep_down * down[0:2]
+        zdown_ref[c] = keep_zdown * buf[c, 0:2]
+        zup_ref[c] = keep_zup * buf[c, 30:32]
 
 
 def pack(velocity):
     comps, depth, width, length = velocity.shape
     ends = jax.ShapeDtypeStruct((comps, 8, 8, length), F32)
     layers = jax.ShapeDtypeStruct((comps, 2, width, length), F32)
-    end_block = pl.BlockSpec((1, 4, 8, length), lambda c, h: (c, h, 0, 0))
-    layer_block = pl.BlockSpec((1, 2, width, length), lambda c, h: (c, 0, 0, 0))
     return pl.pallas_call(
         pack_kernel,
-        grid=(comps, 2),
-        in_specs=[pl.BlockSpec((1, 4, 4, width, length), lambda c, h: (c, 0, h, 0, 0))],
-        out_specs=[end_block] * 2 + [layer_block] * 2,
+        in_specs=[pl.BlockSpec(memory_space=pl.ANY)],
         out_shape=[ends, ends, layers, layers],
+        scratch_shapes=[pltpu.VMEM((comps, depth, width, length), F32), pltpu.SemaphoreType.DMA((comps, 4))],
         compiler_params=pltpu.CompilerParams(vmem_limit_bytes=VMEM_ALL),
         cost_estimate=pl.CostEstimate(flops=2000000, bytes_accessed=9000000, transcendentals=0),
         name="pack",
-    )(velocity.reshape(comps, 4, 8, width, length))
+    )(velocity)
 
 
 def lookup(qcrit, tab_ref):
@@ -311,10 +312,10 @@
     layers, tiles = lax.axis_size("depth"), lax.axis_size("tile")
     table = make_table(sigma_table, color_table, velocity.shape[1] * layers)
     up, down, zup, zdown = pack(velocity)
-    lo = lax.ppermute(up, "tile", shift_up(tiles))
-    hi = lax.ppermute(down, "tile", shift_down(tiles))
-    before = lax.ppermute(zup, "depth", shift_up(layers))
-    after = lax.ppermute(zdown, "depth", shift_down(layers))
+    lo = lax.ppermute(up, "tile", ring(tiles, 1))
+    hi = lax.ppermute(down, "tile", ring(tiles, -1))
+    before = lax.ppermute(zup, "depth", ring(layers, 1))
+    after = lax.ppermute(zdown, "depth", ring(layers, -1))
     comp, edge = middle_pass(velocity, table)
     comp, ends = ends_pass(velocity, before, after, comp, table)
     pieces = edge_pass(edge, ends, lo, hi, comp, table)

time: 47.3 us -> 42.5 us (0.90)
  the two profiles are of different devices: /device:TPU:32 before, /device:TPU:0 now
where the time goes in v3:
time: 42.5 us; the launch traced here: 41.9 us
  Pallas kernels  18.9 us (44%)
  blocking collectives  11.8 us (28%)
  starting transfers between devices  9.42 us (22%)
  waiting for transfers between devices  0.8 us (2%)
  other arithmetic  0.76 us (2%)
    all_to_all x1, blocking collectives, local(): lax.all_to_all(pieces, 'depth', split_axis=0, concat_axis=0, tiled=True)  11.8 us
    pallas_call x1, Pallas kernels, middle_pass(): pl.pallas_call(middle_kernel, grid=(8,), in_specs=[pl.BlockSpec(memory_sp...  10.9 us
    ppermute x1, starting transfers between devices, local(): hi = lax.ppermute(down, 'tile', ring(tiles, -1))  4.82 us
    pallas_call x1, Pallas kernels, pack(): pl.pallas_call(pack_kernel, in_specs=[pl.BlockSpec(memory_space=pl.ANY)],...  3.97 us
    ppermute x1, starting transfers between devices, local(): after = lax.ppermute(zdown, 'depth', ring(layers, -1))  2.95 us
    pallas_call x1, Pallas kernels, ends_pass(): pl.pallas_call(ends_kernel, in_specs=[pl.BlockSpec(memory_space=pl.ANY)]...  2.67 us
    ppermute x1, starting transfers between devices, local(): lo = lax.ppermute(up, 'tile', ring(tiles, 1))  1.64 us
    pallas_call x1, Pallas kernels, edge_pass(): pl.pallas_call(edge_kernel, out_shape=jax.ShapeDtypeStruct((8, 4, width,...  1.32 us
  transfers between devices with their start and end apart: 4, of which 1 were waited for; matrix products, arithmetic and copies ran while one was open for 1% of the time, Pallas kernels for 33%

profile of v3, /device:TPU:0, one launch (start us, length us, event | category | flops | bytes accessed | tf_op | source)
XLA Modules:
  0.0 41.9 jit_solution(18132956352588170526)
XLA Ops:
  0.0 0.0 copy-start.1
  0.0 0.0 copy-start
  0.0 4.0 %pack.1 = (f32[3,8,8,1024]{3,2,1,0:T(8,128)}, f32[3,8,8,1024]{3,2,1,0:T(8,128)S(1)}, f32[3,2,16,1024]{3,2,1,0:T(8,128)}, f32[3,2,16,1024]{3,2,1,0:T(8,128)S(1)}) custom-call(f32[3,32,16,1024]{3,2,1,0:T(8,128)} %v_hbm.5), custom_call_target="tpu_custom_call" | custom-call | flops 2000000 | bytes 9000000 | tf_op jit(solution)/shard_map/pack/pallas_call | solution.py:52
  4.0 1.6 %collective-permute-start.2 = (f32[3,8,8,1024]{3,2,1,0:T(8,128)}, f32[3,8,8,1024]{3,2,1,0:T(8,128)S(1)}, u32[]{:S(2)}, u32[]{:S(2)}) collective-permute-start(f32[3,8,8,1024]{3,2,1,0:T(8,128)} %get-tuple-element.18), channel_id=1, source_target_pairs={{0,1},{1,2},{2,3},{3,4},{4,5},{5,6},{6,7},{7,8},{8,9},{9,10},{10,1... | collective-permute-start | bytes 2359304 | tf_op jit(solution)/shard_map/ppermute | solution.py:315
  5.6 4.8 %collective-permute-start.3 = (f32[3,8,8,1024]{3,2,1,0:T(8,128)S(1)}, f32[3,8,8,1024]{3,2,1,0:T(8,128)S(1)}, u32[]{:S(2)}, u32[]{:S(2)}) collective-permute-start(f32[3,8,8,1024]{3,2,1,0:T(8,128)S(1)} %get-tuple-element.19), channel_id=1, source_target_pairs={{0,15},{1,0},{2,1},{3,2},{4,3},{5,4},{6,5},{7,6},{8,7},{9,8},{10,9... | collective-permute-start | bytes 2359304 | tf_op jit(solution)/shard_map/ppermute | solution.py:316
  10.4 0.0 collective-permute-start
  10.4 3.0 %collective-permute-start.1 = (f32[3,2,16,1024]{3,2,1,0:T(8,128)S(1)}, f32[3,2,16,1024]{3,2,1,0:T(8,128)S(1)}, u32[]{:S(2)}, u32[]{:S(2)}) collective-permute-start(f32[3,2,16,1024]{3,2,1,0:T(8,128)S(1)} %get-tuple-element.15), channel_id=1, source_target_pairs={{0,112},{16,0},{32,16},{48,32},{64,48},{80,64},{96,80},{112,96},{1... | collective-permute-start | bytes 1179656 | tf_op jit(solution)/shard_map/ppermute | solution.py:318
  13.4 0.0 copy-done.1
  13.4 0.0 copy-done
  13.4 0.1 multiply_subtract_fusion
  13.5 0.1 broadcast_in_dim.4
  13.6 0.1 broadcast_in_dim.10.tab_ref
  13.7 10.9 %middle_pass.1 = (f32[4,16,1024]{2,1,0:T(8,128)S(1)}, f32[4,2,8,8,1024]{4,3,2,1,0:T(8,128)S(1)}) custom-call(f32[3,32,16,1024]{3,2,1,0:T(8,128)} %v_hbm.5, f32[16,8,128]{2,1,0:T(8,128)S(1)} %broadcast_in_dim.10.tab_ref), custom_call_target="tpu_custom_call" | custom-call | flops 60000000 | bytes 10000000 | tf_op jit(solution)/shard_map/middle_pass/pallas_call | solution.py:170
  24.6 0.0 collective-permute-done.zlo_ref
  24.6 0.0 collective-permute-done.1.zhi_ref
  24.6 2.7 %ends_pass.1 = (f32[4,16,1024]{2,1,0:T(8,128)S(1)}, f32[4,2,2,8,1024]{4,3,2,1,0:T(8,128)S(1)}) custom-call(f32[3,32,16,1024]{3,2,1,0:T(8,128)} %v_hbm.5, f32[3,2,16,1024]{3,2,1,0:T(8,128)S(1)} %collective-permute-done.zlo_ref, f32[3,2,16,1024]{3,2,1,0:T(8,128)S(1)} %collective-permute-done.1.zhi_ref, f32[4,16,1024]{2,1,0:T(8,128)S(1)} %get-tuple-element.16.comp_ref, ...), custom_call_target="tpu_custom_call" | custom-call | flops 8000000 | bytes 3000000 | tf_op jit(solution)/shard_map/ends_pass/pallas_call | solution.py:238
  27.3 0.8 %collective-permute-done.2.lo_ref = f32[3,8,8,1024]{3,2,1,0:T(8,128)S(1)} collective-permute-done((f32[3,8,8,1024]{3,2,1,0:T(8,128)}, f32[3,8,8,1024]{3,2,1,0:T(8,128)S(1)}, u32[]{:S(2)}, u32[]{:S(2)}) %collective-permute-start.2) | collective-permute-done | bytes 786464 | tf_op jit(solution)/shard_map/ppermute | solution.py:315
  28.1 0.0 collective-permute-done.3.hi_ref
  28.1 1.3 %edge_pass.1 = f32[8,4,16,128]{3,2,1,0:T(8,128)S(1)} custom-call(f32[4,2,8,8,1024]{4,3,2,1,0:T(8,128)S(1)} %get-tuple-element.13.edge_ref, f32[4,2,2,8,1024]{4,3,2,1,0:T(8,128)S(1)} %get-tuple-element.17.ends_ref, f32[3,8,8,1024]{3,2,1,0:T(8,128)S(1)} %collective-permute-done.2.lo_ref, f32[3,8,8,1024]{3,2,1,0:T(8,128)S(1)} %collective-permute-done.3.hi_ref, ...), custom_call_target="tpu_custom_call" | custom-call | flops 10000000 | bytes 4000000 | tf_op jit(solution)/shard_map/edge_pass/pallas_call | solution.py:284
  29.4 11.8 %all_to_all.5 = f32[8,4,16,128]{3,2,1,0:T(8,128)S(1)} all-to-all(f32[8,4,16,128]{3,2,1,0:T(8,128)S(1)} %edge_pass.1), channel_id=1, replica_groups=mesh['depth'=8,'tile'=16] {'depth'}, dimensions={0} | all-to-all | bytes 524288 | tf_op jit(solution)/shard_map/all_to_all | solution.py:322
  41.3 0.6 %pad_maximum_fusion = f32[4,16,128]{2,1,0:T(8,128)} fusion(f32[1,16,128]{2,1,0:T(8,128)S(1)} %get-tuple-element.26, f32[3,16,128]{2,1,0:T(8,128)S(1)} %fusion.13), kind=kLoop, calls=%fused_computation | loop fusion | flops 8192 | bytes 65536 | tf_op jit(solution)/shard_map/concatenate | solution.py:298
  (5 shorter events, 0.1 us)
Async XLA Ops:
  0.0 13.4 %copy-start.1 = (f32[16]{0:T(128)S(1)}, f32[16]{0:T(128)}, u32[]{:S(2)}) copy-start(f32[16]{0:T(128)} %param.4) | copy-start | bytes 196
  0.0 13.4 %copy-start = (f32[3,16]{1,0:T(4,128)S(1)}, f32[3,16]{1,0:T(4,128)}, u32[]{:S(2)}) copy-start(f32[3,16]{1,0:T(4,128)} %param.5) | copy-start | bytes 580
  4.0 24.1 %collective-permute-start.2 = (f32[3,8,8,1024]{3,2,1,0:T(8,128)}, f32[3,8,8,1024]{3,2,1,0:T(8,128)S(1)}, u32[]{:S(2)}, u32[]{:S(2)}) collective-permute-start(f32[3,8,8,1024]{3,2,1,0:T(8,128)} %get-tuple-element.18), channel_id=1, source_target_pairs={{0,1},{1,2},{2,3},{3,4},{4,5},{5,6},{6,7},{7,8},{8,9},{9,10},{10,1... | collective-permute-start | bytes 2359304 | tf_op jit(solution)/shard_map/ppermute | solution.py:315
  5.6 22.5 %collective-permute-start.3 = (f32[3,8,8,1024]{3,2,1,0:T(8,128)S(1)}, f32[3,8,8,1024]{3,2,1,0:T(8,128)S(1)}, u32[]{:S(2)}, u32[]{:S(2)}) collective-permute-start(f32[3,8,8,1024]{3,2,1,0:T(8,128)S(1)} %get-tuple-element.19), channel_id=1, source_target_pairs={{0,15},{1,0},{2,1},{3,2},{4,3},{5,4},{6,5},{7,6},{8,7},{9,8},{10,9... | collective-permute-start | bytes 2359304 | tf_op jit(solution)/shard_map/ppermute | solution.py:316
  10.4 14.2 %collective-permute-start = (f32[3,2,16,1024]{3,2,1,0:T(8,128)}, f32[3,2,16,1024]{3,2,1,0:T(8,128)S(1)}, u32[]{:S(2)}, u32[]{:S(2)}) collective-permute-start(f32[3,2,16,1024]{3,2,1,0:T(8,128)} %get-tuple-element.14), channel_id=1, source_target_pairs={{0,16},{16,32},{32,48},{48,64},{64,80},{80,96},{96,112},{112,0},{1... | collective-permute-start | bytes 1179656 | tf_op jit(solution)/shard_map/ppermute | solution.py:317
  10.4 14.2 %collective-permute-start.1 = (f32[3,2,16,1024]{3,2,1,0:T(8,128)S(1)}, f32[3,2,16,1024]{3,2,1,0:T(8,128)S(1)}, u32[]{:S(2)}, u32[]{:S(2)}) collective-permute-start(f32[3,2,16,1024]{3,2,1,0:T(8,128)S(1)} %get-tuple-element.15), channel_id=1, source_target_pairs={{0,112},{16,0},{32,16},{48,32},{64,48},{80,64},{96,80},{112,96},{1... | collective-permute-start | bytes 1179656 | tf_op jit(solution)/shard_map/ppermute | solution.py:318

commit v4 on v3

--- a/solution.py
+++ b/solution.py
@@ -249,53 +249,69 @@
     )(velocity, before, after, comp, table)
 
 
-def edge_kernel(edge_ref, ends_ref, lo_ref, hi_ref, comp_ref, tab_ref, out_ref):
+def edge_kernel(edge_ref, ends_ref, lo_ref, hi_ref, comp_ref, tab_ref, mine_ref, other_ref):
     row = lax.broadcasted_iota(jnp.int32, (8, 128), 0)
     first, last = row < 2, row > 5
-    for j in range(8):
-        lanes = slice(j * 128, j * 128 + 128)
-        out_ref[j] = comp_ref[:, :, lanes]
-        for side, halo_ref in enumerate((lo_ref, hi_ref)):
-            zeros = jnp.zeros((8, 128), F32)
-            carry = (zeros + 1.0, [zeros] * 3)
-            for zz in range(8):
-                terms = [edge_ref[e, side, zz, :, lanes] for e in range(4)]
-                if zz < 2:
-                    terms = [jnp.where(first, ends_ref[e, side, zz, :, lanes], t) for e, t in enumerate(terms)]
-                if zz > 5:
-                    terms = [jnp.where(last, ends_ref[e, side, zz - 6, :, lanes], t) for e, t in enumerate(terms)]
-                part, by_z, by_x, by_y = terms
-                hz, hx, hy = [halo_ref[c, zz, :, lanes] for c in range(3)]
-                total = part + by_z * hz + by_y * hy + hx * (by_x + hx)
-                step, colors = lookup(QSCALE * total, tab_ref)
-                carry = composite(carry, step, colors)
-            trans, shades = carry
-            for back in (2, 4):
-                shades = [s + trans * pltpu.roll(s, 8 - back, 0) for s in shades]
-                trans = trans * pltpu.roll(trans, 8 - back, 0)
-            start = 14 * side
-            for c in range(3):
-                out_ref[j, c, start : start + 2, :] = shades[c][0:2]
-            out_ref[j, 3, start : start + 2, :] = trans[0:2]
+    core = lax.rem(lax.axis_index("depth"), 2)
+    for slot, out_ref in enumerate((mine_ref, other_ref)):
+        for k in range(4):
+            piece = 2 * k + lax.rem(core + slot, 2)
+            lanes = pl.ds(pl.multiple_of(piece * 128, 128), 128)
+            out_ref[k] = comp_ref[:, :, lanes]
+            for side, halo_ref in enumerate((lo_ref, hi_ref)):
+                zeros = jnp.zeros((8, 128), F32)
+                carry = (zeros + 1.0, [zeros] * 3)
+                for zz in range(8):
+                    terms = [edge_ref[e, side, zz, :, lanes] for e in range(4)]
+                    if zz < 2:
+                        terms = [jnp.where(first, ends_ref[e, side, zz, :, lanes], t) for e, t in enumerate(terms)]
+                    if zz > 5:
+                        terms = [jnp.where(last, ends_ref[e, side, zz - 6, :, lanes], t) for e, t in enumerate(terms)]
+                    part, by_z, by_x, by_y = terms
+                    hz, hx, hy = [halo_ref[c, zz, :, lanes] for c in range(3)]
+                    total = part + by_z * hz + by_y * hy + hx * (by_x + hx)
+                    step, colors = lookup(QSCALE * total, tab_ref)
+                    carry = composite(carry, step, colors)
+                trans, shades = carry
+                for back in (2, 4):
+                    shades = [s + trans * pltpu.roll(s, 8 - back, 0) for s in shades]
+                    trans = trans * pltpu.roll(trans, 8 - back, 0)
+                start = 14 * side
+                for c in range(3):
+                    out_ref[k, c, start : start + 2, :] = shades[c][0:2]
+                out_ref[k, 3, start : start + 2, :] = trans[0:2]
 
 
 def edge_pass(edge, ends, lo, hi, comp, table):
-    width = comp.shape[1]
+    pieces = jax.ShapeDtypeStruct((4, 4, comp.shape[1], 128), F32)
     return pl.pallas_call(
         edge_kernel,
-        out_shape=jax.ShapeDtypeStruct((8, 4, width, 128), F32),
+        out_shape=[pieces, pieces],
         compiler_params=pltpu.CompilerParams(vmem_limit_bytes=VMEM_LIMIT),
         cost_estimate=pl.CostEstimate(flops=10000000, bytes_accessed=4000000, transcendentals=300000),
         name="edge_pass",
     )(edge, ends, lo, hi, comp, table)
 
 
-def over(parts):
-    result = parts[7]
-    for layer in range(6, -1, -1):
-        front = parts[layer]
-        shade = front[:3] + front[3:] * result[:3]
-        result = jnp.concatenate([shade, front[3:] * result[3:]], axis=0)
+def over(front, back):
+    shade = front[..., :3, :, :] + front[..., 3:, :, :] * back[..., :3, :, :]
+    return jnp.concatenate([shade, front[..., 3:, :, :] * back[..., 3:, :, :]], axis=-3)
+
+
+def gather_over(mine, other):
+    place = lax.axis_index("depth")
+    core, chip = lax.rem(place, 2), lax.div(place, 2)
+    got = lax.ppermute(other, "depth", [(i, i ^ 1) for i in range(8)])
+    near = core == 0
+    pair = over(jnp.where(near, mine, got), jnp.where(near, got, mine))
+    parts = [lax.dynamic_index_in_dim(pair, chip, 0, keepdims=False)]
+    for k in range(1, 4):
+        piece = lax.dynamic_index_in_dim(pair, lax.rem(chip + k, 4), 0, keepdims=False)
+        parts.append(lax.ppermute(piece, "depth", ring(8, 2 * k)))
+    parts = jnp.stack(parts)
+    result = lax.dynamic_index_in_dim(parts, lax.rem(chip + 1, 4), 0, keepdims=False)
+    for source in (2, 1, 0):
+        result = over(lax.dynamic_index_in_dim(parts, lax.rem(chip + 4 - source, 4), 0, keepdims=False), result)
     return result
 
 
@@ -318,9 +334,8 @@
     after = lax.ppermute(zdown, "depth", ring(layers, -1))
     comp, edge = middle_pass(velocity, table)
     comp, ends = ends_pass(velocity, before, after, comp, table)
-    pieces = edge_pass(edge, ends, lo, hi, comp, table)
-    received = lax.all_to_all(pieces, "depth", split_axis=0, concat_axis=0, tiled=True)
-    return over(received)
+    mine, other = edge_pass(edge, ends, lo, hi, comp, table)
+    return gather_over(mine, other)
 
 
 def solution(mesh):

time: 42.5 us -> 40.3 us (0.948); the launches traced: 41.9 us -> 40.2 us
  blocking collectives: 11.8 us -> 0 us
  starting transfers between devices: 9.42 us -> 15.4 us
  waiting for transfers between devices: 0.8 us -> 4.65 us
    all_to_all x1 -> x0, blocking collectives: 11.8 us -> none  [local(): lax.all_to_all(pieces, 'depth', split_axis=0, concat_axis=0, tiled=True)]
    ppermute x0 -> x4, starting transfers between devices: none -> 5.98 us  [the longest x3 5.89 us: gather_over(): parts.append(lax.ppermute(piece, 'depth', ring(8, 2 * k)))]
    ppermute x0 -> x4, waiting for transfers between devices: none -> 3.84 us  [the longest x3 2.56 us: gather_over(): parts.append(lax.ppermute(piece, 'depth', ring(8, 2 * k)))]
  transfers between devices with their start and end apart: 4 -> 8, of which waited for: 1 -> 4; matrix products, arithmetic and copies ran while one was open for 1% -> 1% of each run, Pallas kernels for 33% -> 34%
where the time goes in v4:
time: 40.3 us; the launch traced here: 40.2 us
  Pallas kernels  19 us (47%)
  starting transfers between devices  15.4 us (38%)
  waiting for transfers between devices  4.65 us (12%)
  other arithmetic  0.85 us (2%)
    pallas_call x1, Pallas kernels, middle_pass(): pl.pallas_call(middle_kernel, grid=(8,), in_specs=[pl.BlockSpec(memory_sp...  10.9 us
    ppermute x3, starting transfers between devices, gather_over(): parts.append(lax.ppermute(piece, 'depth', ring(8, 2 * k)))  5.89 us
    ppermute x1, starting transfers between devices, local(): hi = lax.ppermute(down, 'tile', ring(tiles, -1))  4.82 us
    pallas_call x1, Pallas kernels, pack(): pl.pallas_call(pack_kernel, in_specs=[pl.BlockSpec(memory_space=pl.ANY)],...  4 us
    ppermute x1, starting transfers between devices, local(): after = lax.ppermute(zdown, 'depth', ring(layers, -1))  2.95 us
    pallas_call x1, Pallas kernels, ends_pass(): pl.pallas_call(ends_kernel, in_specs=[pl.BlockSpec(memory_space=pl.ANY)]...  2.67 us
    ppermute x3, waiting for transfers between devices, gather_over(): parts.append(lax.ppermute(piece, 'depth', ring(8, 2 * k)))  2.56 us
    ppermute x1, starting transfers between devices, local(): lo = lax.ppermute(up, 'tile', ring(tiles, 1))  1.64 us
  transfers between devices with their start and end apart: 8, of which 4 were waited for; matrix products, arithmetic and copies ran while one was open for 1% of the time, Pallas kernels for 34%

profile of v4, /device:TPU:0, one launch (start us, length us, event | category | flops | bytes accessed | tf_op | source)
XLA Modules:
  0.0 40.2 jit_solution(6032324510414916665)
XLA Ops:
  0.0 0.0 copy-start.1
  0.0 0.0 copy-start
  0.0 4.0 %pack.1 = (f32[3,8,8,1024]{3,2,1,0:T(8,128)}, f32[3,8,8,1024]{3,2,1,0:T(8,128)S(1)}, f32[3,2,16,1024]{3,2,1,0:T(8,128)}, f32[3,2,16,1024]{3,2,1,0:T(8,128)S(1)}) custom-call(f32[3,32,16,1024]{3,2,1,0:T(8,128)} %v_hbm.5), custom_call_target="tpu_custom_call" | custom-call | flops 2000000 | bytes 9000000 | tf_op jit(solution)/shard_map/pack/pallas_call | solution.py:52
  4.0 1.6 %collective-permute-start.2 = (f32[3,8,8,1024]{3,2,1,0:T(8,128)}, f32[3,8,8,1024]{3,2,1,0:T(8,128)S(1)}, u32[]{:S(2)}, u32[]{:S(2)}) collective-permute-start(f32[3,8,8,1024]{3,2,1,0:T(8,128)} %get-tuple-element.20), channel_id=1, source_target_pairs={{0,1},{1,2},{2,3},{3,4},{4,5},{5,6},{6,7},{7,8},{8,9},{9,10},{10,1... | collective-permute-start | bytes 2359304 | tf_op jit(solution)/shard_map/ppermute | solution.py:331
  5.7 4.8 %collective-permute-start.3 = (f32[3,8,8,1024]{3,2,1,0:T(8,128)S(1)}, f32[3,8,8,1024]{3,2,1,0:T(8,128)S(1)}, u32[]{:S(2)}, u32[]{:S(2)}) collective-permute-start(f32[3,8,8,1024]{3,2,1,0:T(8,128)S(1)} %get-tuple-element.21), channel_id=1, source_target_pairs={{0,15},{1,0},{2,1},{3,2},{4,3},{5,4},{6,5},{7,6},{8,7},{9,8},{10,9... | collective-permute-start | bytes 2359304 | tf_op jit(solution)/shard_map/ppermute | solution.py:332
  10.5 0.0 collective-permute-start
  10.5 3.0 %collective-permute-start.1 = (f32[3,2,16,1024]{3,2,1,0:T(8,128)S(1)}, f32[3,2,16,1024]{3,2,1,0:T(8,128)S(1)}, u32[]{:S(2)}, u32[]{:S(2)}) collective-permute-start(f32[3,2,16,1024]{3,2,1,0:T(8,128)S(1)} %get-tuple-element.17), channel_id=1, source_target_pairs={{0,112},{16,0},{32,16},{48,32},{64,48},{80,64},{96,80},{112,96},{1... | collective-permute-start | bytes 1179656 | tf_op jit(solution)/shard_map/ppermute | solution.py:334
  13.4 0.0 copy-done.1
  13.4 0.0 copy-done
  13.5 0.1 multiply_subtract_fusion
  13.5 0.1 broadcast_in_dim.4
  13.6 0.1 broadcast_in_dim.10.tab_ref
  13.7 10.9 %middle_pass.1 = (f32[4,16,1024]{2,1,0:T(8,128)S(1)}, f32[4,2,8,8,1024]{4,3,2,1,0:T(8,128)S(1)}) custom-call(f32[3,32,16,1024]{3,2,1,0:T(8,128)} %v_hbm.5, f32[16,8,128]{2,1,0:T(8,128)S(1)} %broadcast_in_dim.10.tab_ref), custom_call_target="tpu_custom_call" | custom-call | flops 60000000 | bytes 10000000 | tf_op jit(solution)/shard_map/middle_pass/pallas_call | solution.py:170
  24.7 0.0 collective-permute-done.zlo_ref
  24.7 0.0 collective-permute-done.1.zhi_ref
  24.7 2.7 %ends_pass.1 = (f32[4,16,1024]{2,1,0:T(8,128)S(1)}, f32[4,2,2,8,1024]{4,3,2,1,0:T(8,128)S(1)}) custom-call(f32[3,32,16,1024]{3,2,1,0:T(8,128)} %v_hbm.5, f32[3,2,16,1024]{3,2,1,0:T(8,128)S(1)} %collective-permute-done.zlo_ref, f32[3,2,16,1024]{3,2,1,0:T(8,128)S(1)} %collective-permute-done.1.zhi_ref, f32[4,16,1024]{2,1,0:T(8,128)S(1)} %get-tuple-element.18.comp_ref, ...), custom_call_target="tpu_custom_call" | custom-call | flops 8000000 | bytes 3000000 | tf_op jit(solution)/shard_map/ends_pass/pallas_call | solution.py:238
  27.4 0.8 %collective-permute-done.2.lo_ref = f32[3,8,8,1024]{3,2,1,0:T(8,128)S(1)} collective-permute-done((f32[3,8,8,1024]{3,2,1,0:T(8,128)}, f32[3,8,8,1024]{3,2,1,0:T(8,128)S(1)}, u32[]{:S(2)}, u32[]{:S(2)}) %collective-permute-start.2) | collective-permute-done | bytes 786464 | tf_op jit(solution)/shard_map/ppermute | solution.py:331
  28.2 0.0 collective-permute-done.3.hi_ref
  28.2 1.4 %edge_pass.1 = (f32[4,4,16,128]{3,2,1,0:T(8,128)S(1)}, f32[4,4,16,128]{3,2,1,0:T(8,128)S(1)}) custom-call(f32[4,2,8,8,1024]{4,3,2,1,0:T(8,128)S(1)} %get-tuple-element.15.edge_ref, f32[4,2,2,8,1024]{4,3,2,1,0:T(8,128)S(1)} %get-tuple-element.19.ends_ref, f32[3,8,8,1024]{3,2,1,0:T(8,128)S(1)} %collective-permute-done.2.lo_ref, ...), custom_call_target="tpu_custom_call" | custom-call | flops 10000000 | bytes 4000000 | tf_op jit(solution)/shard_map/edge_pass/pallas_call | solution.py:287
  29.5 0.1 collective-permute-start.4
  29.7 1.3 %collective-permute-done.4 = f32[4,4,16,128]{3,2,1,0:T(8,128)S(1)} collective-permute-done((f32[4,4,16,128]{3,2,1,0:T(8,128)S(1)}, f32[4,4,16,128]{3,2,1,0:T(8,128)S(1)}, u32[]{:S(2)}, u32[]{:S(2)}) %collective-permute-start.4) | collective-permute-done | bytes 131104 | tf_op jit(solution)/shard_map/ppermute | solution.py:304
  31.1 1.6 %collective-permute-start.5 = (f32[4,16,128]{2,1,0:T(8,128)S(1)}, f32[4,16,128]{2,1,0:T(8,128)S(1)}, u32[]{:S(2)}, u32[]{:S(2)}) collective-permute-start(f32[4,16,128]{2,1,0:T(8,128)S(1)} %get-tuple-element.34), channel_id=1, source_target_pairs={{0,32},{16,48},{32,64},{48,80},{64,96},{80,112},{96,0},{112,16},{1... | collective-permute-start | bytes 98312 | tf_op jit(solution)/shard_map/ppermute | solution.py:310
  32.7 2.9 %collective-permute-start.6 = (f32[4,16,128]{2,1,0:T(8,128)S(1)}, f32[4,16,128]{2,1,0:T(8,128)S(1)}, u32[]{:S(2)}, u32[]{:S(2)}) collective-permute-start(f32[4,16,128]{2,1,0:T(8,128)S(1)} %get-tuple-element.35), channel_id=1, source_target_pairs={{0,64},{16,80},{32,96},{48,112},{64,0},{80,16},{96,32},{112,48},{1... | collective-permute-start | bytes 98312 | tf_op jit(solution)/shard_map/ppermute | solution.py:310
  35.6 1.3 %collective-permute-start.7 = (f32[4,16,128]{2,1,0:T(8,128)S(1)}, f32[4,16,128]{2,1,0:T(8,128)S(1)}, u32[]{:S(2)}, u32[]{:S(2)}) collective-permute-start(f32[4,16,128]{2,1,0:T(8,128)S(1)} %get-tuple-element.36), channel_id=1, source_target_pairs={{0,96},{16,112},{32,0},{48,16},{64,32},{80,48},{96,64},{112,80},{1... | collective-permute-start | bytes 98312 | tf_op jit(solution)/shard_map/ppermute | solution.py:310
  36.9 0.0 collective-permute-done.5
  37.0 1.2 %collective-permute-done.6 = f32[4,16,128]{2,1,0:T(8,128)S(1)} collective-permute-done((f32[4,16,128]{2,1,0:T(8,128)S(1)}, f32[4,16,128]{2,1,0:T(8,128)S(1)}, u32[]{:S(2)}, u32[]{:S(2)}) %collective-permute-start.6) | collective-permute-done | bytes 32800 | tf_op jit(solution)/shard_map/ppermute | solution.py:310
  38.1 1.4 %collective-permute-done.7 = f32[4,16,128]{2,1,0:T(8,128)S(1)} collective-permute-done((f32[4,16,128]{2,1,0:T(8,128)S(1)}, f32[4,16,128]{2,1,0:T(8,128)S(1)}, u32[]{:S(2)}, u32[]{:S(2)}) %collective-permute-start.7) | collective-permute-done | bytes 32800 | tf_op jit(solution)/shard_map/ppermute | solution.py:310
  39.6 0.6 %pad_maximum_fusion.1 = f32[4,16,128]{2,1,0:T(8,128)} fusion(f32[1,16,128]{2,1,0:T(8,128)S(1)} %get-tuple-element.30, f32[3,16,128]{2,1,0:T(8,128)S(1)} %fusion.13), kind=kLoop, calls=%fused_computation.21 | loop fusion | flops 8192 | bytes 65536 | tf_op jit(solution)/shard_map/concatenate | solution.py:298
  (10 shorter events, 0.2 us)
Async XLA Ops:
  0.0 13.4 %copy-start.1 = (f32[16]{0:T(128)S(1)}, f32[16]{0:T(128)}, u32[]{:S(2)}) copy-start(f32[16]{0:T(128)} %param.4) | copy-start | bytes 196
  0.0 13.4 %copy-start = (f32[3,16]{1,0:T(4,128)S(1)}, f32[3,16]{1,0:T(4,128)}, u32[]{:S(2)}) copy-start(f32[3,16]{1,0:T(4,128)} %param.5) | copy-start | bytes 580
  4.0 24.1 %collective-permute-start.2 = (f32[3,8,8,1024]{3,2,1,0:T(8,128)}, f32[3,8,8,1024]{3,2,1,0:T(8,128)S(1)}, u32[]{:S(2)}, u32[]{:S(2)}) collective-permute-start(f32[3,8,8,1024]{3,2,1,0:T(8,128)} %get-tuple-element.20), channel_id=1, source_target_pairs={{0,1},{1,2},{2,3},{3,4},{4,5},{5,6},{6,7},{7,8},{8,9},{9,10},{10,1... | collective-permute-start | bytes 2359304 | tf_op jit(solution)/shard_map/ppermute | solution.py:331
  5.7 22.5 %collective-permute-start.3 = (f32[3,8,8,1024]{3,2,1,0:T(8,128)S(1)}, f32[3,8,8,1024]{3,2,1,0:T(8,128)S(1)}, u32[]{:S(2)}, u32[]{:S(2)}) collective-permute-start(f32[3,8,8,1024]{3,2,1,0:T(8,128)S(1)} %get-tuple-element.21), channel_id=1, source_target_pairs={{0,15},{1,0},{2,1},{3,2},{4,3},{5,4},{6,5},{7,6},{8,7},{9,8},{10,9... | collective-permute-start | bytes 2359304 | tf_op jit(solution)/shard_map/ppermute | solution.py:332
  10.5 14.2 %collective-permute-start = (f32[3,2,16,1024]{3,2,1,0:T(8,128)}, f32[3,2,16,1024]{3,2,1,0:T(8,128)S(1)}, u32[]{:S(2)}, u32[]{:S(2)}) collective-permute-start(f32[3,2,16,1024]{3,2,1,0:T(8,128)} %get-tuple-element.16), channel_id=1, source_target_pairs={{0,16},{16,32},{32,48},{48,64},{64,80},{80,96},{96,112},{112,0},{1... | collective-permute-start | bytes 1179656 | tf_op jit(solution)/shard_map/ppermute | solution.py:333
  10.5 14.2 %collective-permute-start.1 = (f32[3,2,16,1024]{3,2,1,0:T(8,128)S(1)}, f32[3,2,16,1024]{3,2,1,0:T(8,128)S(1)}, u32[]{:S(2)}, u32[]{:S(2)}) collective-permute-start(f32[3,2,16,1024]{3,2,1,0:T(8,128)S(1)} %get-tuple-element.17), channel_id=1, source_target_pairs={{0,112},{16,0},{32,16},{48,32},{64,48},{80,64},{96,80},{112,96},{1... | collective-permute-start | bytes 1179656 | tf_op jit(solution)/shard_map/ppermute | solution.py:334
  29.5 1.4 %collective-permute-start.4 = (f32[4,4,16,128]{3,2,1,0:T(8,128)S(1)}, f32[4,4,16,128]{3,2,1,0:T(8,128)S(1)}, u32[]{:S(2)}, u32[]{:S(2)}) collective-permute-start(f32[4,4,16,128]{3,2,1,0:T(8,128)S(1)} %get-tuple-element.24), channel_id=1, source_target_pairs={{0,16},{16,0},{32,48},{48,32},{64,80},{80,64},{96,112},{112,96},{1... | collective-permute-start | bytes 393224 | tf_op jit(solution)/shard_map/ppermute | solution.py:304
  31.1 5.9 %collective-permute-start.5 = (f32[4,16,128]{2,1,0:T(8,128)S(1)}, f32[4,16,128]{2,1,0:T(8,128)S(1)}, u32[]{:S(2)}, u32[]{:S(2)}) collective-permute-start(f32[4,16,128]{2,1,0:T(8,128)S(1)} %get-tuple-element.34), channel_id=1, source_target_pairs={{0,32},{16,48},{32,64},{48,80},{64,96},{80,112},{96,0},{112,16},{1... | collective-permute-start | bytes 98312 | tf_op jit(solution)/shard_map/ppermute | solution.py:310
  32.7 5.4 %collective-permute-start.6 = (f32[4,16,128]{2,1,0:T(8,128)S(1)}, f32[4,16,128]{2,1,0:T(8,128)S(1)}, u32[]{:S(2)}, u32[]{:S(2)}) collective-permute-start(f32[4,16,128]{2,1,0:T(8,128)S(1)} %get-tuple-element.35), channel_id=1, source_target_pairs={{0,64},{16,80},{32,96},{48,112},{64,0},{80,16},{96,32},{112,48},{1... | collective-permute-start | bytes 98312 | tf_op jit(solution)/shard_map/ppermute | solution.py:310
  35.6 3.9 %collective-permute-start.7 = (f32[4,16,128]{2,1,0:T(8,128)S(1)}, f32[4,16,128]{2,1,0:T(8,128)S(1)}, u32[]{:S(2)}, u32[]{:S(2)}) collective-permute-start(f32[4,16,128]{2,1,0:T(8,128)S(1)} %get-tuple-element.36), channel_id=1, source_target_pairs={{0,96},{16,112},{32,0},{48,16},{64,32},{80,48},{96,64},{112,80},{1... | collective-permute-start | bytes 98312 | tf_op jit(solution)/shard_map/ppermute | solution.py:310

commit v5 on v4

--- a/solution.py
+++ b/solution.py
@@ -6,8 +6,8 @@
 from jax.sharding import PartitionSpec as P
 
 F32 = jnp.float32
-VMEM_LIMIT = 40 * 1024 * 1024
-VMEM_ALL = 50 * 1024 * 1024
+VMEM_LIMIT = 20 * 1024 * 1024
+VMEM_ALL = 44 * 1024 * 1024
 QSCALE = -1.0 / 1152.0
 
 
@@ -15,14 +15,24 @@
     return [(i, (i + by) % count) for i in range(count)]
 
 
-def pack_kernel(v_hbm, up_ref, down_ref, zup_ref, zdown_ref, buf, sems):
+def pack_kernel(v_hbm, held_ref, up_ref, down_ref, zup_ref, zdown_ref, sems):
+    length = v_hbm.shape[3]
     copies = [
-        [pltpu.make_async_copy(v_hbm.at[c, 8 * q : 8 * q + 8], buf.at[c, 8 * q : 8 * q + 8], sems.at[c, q]) for q in range(4)]
+        [
+            pltpu.make_async_copy(
+                v_hbm.at[c, 8 * q : 8 * q + 8], held_ref.at[c, 8 * q : 8 * q + 8, :, 128 : 128 + length], sems.at[c, q]
+            )
+            for q in range(4)
+        ]
         for c in range(3)
     ]
     for some in copies:
         for copy in some:
             copy.start()
+    zeros = jnp.zeros(held_ref.shape[:3] + (128,), F32)
+    held_ref[:, :, :, 0:128] = zeros
+    held_ref[:, :, :, 128 + length :] = zeros
+    inner = slice(128, 128 + length)
     tile, tiles = lax.axis_index("tile"), lax.axis_size("tile")
     layer, layers = lax.axis_index("depth"), lax.axis_size("depth")
     keep_up = jnp.where(tile == tiles - 1, 0.0, 1.0)
@@ -35,14 +45,14 @@
             copies[c][quarter].wait()
             for zz in range(8):
                 z = quarter * 8 + zz
-                low = buf[c, z, 0:8, :]
-                high = buf[c, z, 8:16, :]
+                low = held_ref[c, z, 0:8, inner]
+                high = held_ref[c, z, 8:16, inner]
                 up = jnp.where(row == 6, high - 8.0 * pltpu.roll(high, 7, 0), high)
                 down = jnp.where(row == 0, -low, 8.0 * pltpu.roll(low, 1, 0) - low)
                 up_ref[c, zz, 2 * quarter : 2 * quarter + 2, :] = keep_up * up[6:8]
                 down_ref[c, zz, 2 * quarter : 2 * quarter + 2, :] = keep_down * down[0:2]
-        zdown_ref[c] = keep_zdown * buf[c, 0:2]
-        zup_ref[c] = keep_zup * buf[c, 30:32]
+        zdown_ref[c] = keep_zdown * held_ref[c, 0:2, :, inner]
+        zup_ref[c] = keep_zup * held_ref[c, 30:32, :, inner]
 
 
 def pack(velocity):
@@ -52,8 +62,8 @@
     return pl.pallas_call(
         pack_kernel,
         in_specs=[pl.BlockSpec(memory_space=pl.ANY)],
-        out_shape=[ends, ends, layers, layers],
-        scratch_shapes=[pltpu.VMEM((comps, depth, width, length), F32), pltpu.SemaphoreType.DMA((comps, 4))],
+        out_shape=[pltpu.VMEM((comps, depth, width, length + 256), F32), ends, ends, layers, layers],
+        scratch_shapes=[pltpu.SemaphoreType.DMA((comps, 4))],
         compiler_params=pltpu.CompilerParams(vmem_limit_bytes=VMEM_ALL),
         cost_estimate=pl.CostEstimate(flops=2000000, bytes_accessed=9000000, transcendentals=0),
         name="pack",
@@ -113,89 +123,62 @@
     return total, 2.0 * dz[1], 2.0 * dx[1], 2.0 * dy[1]
 
 
-def middle_kernel(v_hbm, tab_ref, comp_ref, edge_ref, buf, sems):
-    j = pl.program_id(0)
-
-    def copy(k):
-        lanes = pl.ds(pl.multiple_of(k * 128, 128), 128)
-        inner = pl.ds(pl.multiple_of((k + 1) * 128, 128), 128)
-        return pltpu.make_async_copy(v_hbm.at[:, :, :, lanes], buf.at[:, :, :, inner], sems.at[k])
-
-    @pl.when(j == 0)
-    def _():
-        for k in range(8):
-            copy(k).start()
-        zeros = jnp.zeros((3, 32, 16, 128), F32)
-        buf[:, :, :, 0:128] = zeros
-        buf[:, :, :, 9 * 128 : 10 * 128] = zeros
-        copy(0).wait()
-
-    @pl.when(j < 7)
-    def _():
-        copy(j + 1).wait()
-
+def middle_kernel(held_ref, tab_ref, comp_ref, edge_ref):
     masks = edge_masks()
-    left = pl.ds(pl.multiple_of(j * 128, 128), 128)
-    mid = pl.ds(pl.multiple_of(j * 128 + 128, 128), 128)
-    right = pl.ds(pl.multiple_of(j * 128 + 256, 128), 128)
-    for side in range(2):
-        rows = slice(8 * side, 8 * side + 8)
-        others = slice(8 - 8 * side, 16 - 8 * side)
-        zeros = jnp.zeros((8, 128), F32)
-        carry = (zeros + 1.0, [zeros] * 3)
-        lines = [[buf[c, z, rows, mid] for z in range(32)] for c in range(3)]
-        for z in range(2, 30):
-            quarter, zz = z // 8, z % 8
-            dz, dx, dy = gradients(
-                [lines[c][z - 2 : z + 3] for c in range(3)],
-                [buf[c, z, others, mid] for c in range(3)],
-                [buf[c, z, rows, left] for c in range(3)],
-                [buf[c, z, rows, right] for c in range(3)],
-                side,
-                masks,
-            )
-            total = invariant(dz, dx, dy)
-            ends = slice(6 * side, 6 * side + 2)
-            for e, value in enumerate(edge_terms(total, dz, dx, dy)):
-                edge_ref[e, side, zz, 2 * quarter : 2 * quarter + 2, :] = value[ends]
-            step, colors = lookup(QSCALE * total, tab_ref)
-            carry = composite(carry, step, colors)
-        for c in range(3):
-            comp_ref[c, rows, :] = carry[1][c]
-        comp_ref[3, rows, :] = carry[0]
-
-
-def middle_pass(velocity, table):
-    comps, depth, width, length = velocity.shape
+
+    @pl.loop(0, 8)
+    def _(j):
+        left = pl.ds(pl.multiple_of(j * 128, 128), 128)
+        mid = pl.ds(pl.multiple_of(j * 128 + 128, 128), 128)
+        right = pl.ds(pl.multiple_of(j * 128 + 256, 128), 128)
+        for side in range(2):
+            rows = slice(8 * side, 8 * side + 8)
+            others = slice(8 - 8 * side, 16 - 8 * side)
+            zeros = jnp.zeros((8, 128), F32)
+            carry = (zeros + 1.0, [zeros] * 3)
+            lines = [[held_ref[c, z, rows, mid] for z in range(32)] for c in range(3)]
+            for z in range(2, 30):
+                quarter, zz = z // 8, z % 8
+                dz, dx, dy = gradients(
+                    [lines[c][z - 2 : z + 3] for c in range(3)],
+                    [held_ref[c, z, others, mid] for c in range(3)],
+                    [held_ref[c, z, rows, left] for c in range(3)],
+                    [held_ref[c, z, rows, right] for c in range(3)],
+                    side,
+                    masks,
+                )
+                total = invariant(dz, dx, dy)
+                ends = slice(6 * side, 6 * side + 2)
+                for e, value in enumerate(edge_terms(total, dz, dx, dy)):
+                    edge_ref[e, side, zz, 2 * quarter : 2 * quarter + 2, left] = value[ends]
+                step, colors = lookup(QSCALE * total, tab_ref)
+                carry = composite(carry, step, colors)
+            for c in range(3):
+                comp_ref[c, rows, left] = carry[1][c]
+            comp_ref[3, rows, left] = carry[0]
+
+
+def middle_pass(held, table):
+    comps, depth, width, length = held.shape
+    length -= 256
     return pl.pallas_call(
         middle_kernel,
-        grid=(8,),
-        in_specs=[pl.BlockSpec(memory_space=pl.ANY), pl.BlockSpec((16, 8, 128), lambda j: (0, 0, 0))],
-        out_specs=[
-            pl.BlockSpec((4, width, 128), lambda j: (0, 0, j)),
-            pl.BlockSpec((4, 2, 8, 8, 128), lambda j: (0, 0, 0, 0, j)),
-        ],
         out_shape=[
             jax.ShapeDtypeStruct((4, width, length), F32),
             jax.ShapeDtypeStruct((4, 2, 8, 8, length), F32),
         ],
-        scratch_shapes=[pltpu.VMEM((comps, depth, width, length + 256), F32), pltpu.SemaphoreType.DMA((8,))],
-        compiler_params=pltpu.CompilerParams(vmem_limit_bytes=VMEM_ALL),
+        compiler_params=pltpu.CompilerParams(vmem_limit_bytes=VMEM_LIMIT),
         cost_estimate=pl.CostEstimate(flops=60000000, bytes_accessed=10000000, transcendentals=1000000),
         name="middle_pass",
-    )(velocity, table)
-
-
-def ends_kernel(v_hbm, zlo_ref, zhi_ref, comp_ref, tab_ref, out_ref, edge_ref, buf, sems):
-    copies = [pltpu.make_async_copy(v_hbm.at[:, 28 * k : 28 * k + 4], buf.at[k], sems.at[k]) for k in range(2)]
-    for copy in copies:
-        copy.start()
-    for copy in copies:
-        copy.wait()
+    )(held, table)
+
+
+def ends_kernel(held_ref, zlo_ref, zhi_ref, comp_ref, tab_ref, out_ref, edge_ref):
     masks = edge_masks()
     zeros = jnp.zeros((8, 128), F32)
     for j in range(8):
         lanes = slice(j * 128, j * 128 + 128)
+        left, mid, right = [slice(j * 128 + m, j * 128 + m + 128) for m in (0, 128, 256)]
         for side in range(2):
             rows = slice(8 * side, 8 * side + 8)
             others = slice(8 - 8 * side, 16 - 8 * side)
@@ -203,17 +186,14 @@
             for k in range(2):
                 first = [[zlo_ref[c, i, rows, lanes] for i in range(2)] for c in range(3)] if k == 0 else [[]] * 3
                 last = [[zhi_ref[c, i, rows, lanes] for i in range(2)] for c in range(3)] if k == 1 else [[]] * 3
-                lines = [first[c] + [buf[k, c, i, rows, lanes] for i in range(4)] + last[c] for c in range(3)]
+                lines = [first[c] + [held_ref[c, 28 * k + i, rows, mid] for i in range(4)] + last[c] for c in range(3)]
                 for i in range(2):
-                    at = i + 2 * k
-                    sideways = lambda m: [
-                        buf[k, c, at, rows, m * 128 : m * 128 + 128] if 0 <= m < 8 else zeros for c in range(3)
-                    ]
+                    at = 30 * k + i
                     dz, dx, dy = gradients(
                         [lines[c][i : i + 5] for c in range(3)],
-                        [buf[k, c, at, others, lanes] for c in range(3)],
-                        sideways(j - 1),
-                        sideways(j + 1),
+                        [held_ref[c, at, others, mid] for c in range(3)],
+                        [held_ref[c, at, rows, left] for c in range(3)],
+                        [held_ref[c, at, rows, right] for c in range(3)],
                         side,
                         masks,
                     )
@@ -232,21 +212,18 @@
             out_ref[3, rows, lanes] = carry[0]
 
 
-def ends_pass(velocity, before, after, comp, table):
-    comps, depth, width, length = velocity.shape
-    vmem = pl.BlockSpec(memory_space=pltpu.VMEM)
+def ends_pass(held, before, after, comp, table):
+    width, length = comp.shape[1:]
     return pl.pallas_call(
         ends_kernel,
-        in_specs=[pl.BlockSpec(memory_space=pl.ANY)] + [vmem] * 4,
         out_shape=[
             jax.ShapeDtypeStruct((4, width, length), F32),
             jax.ShapeDtypeStruct((4, 2, 2, 8, length), F32),
         ],
-        scratch_shapes=[pltpu.VMEM((2, comps, 4, width, length), F32), pltpu.SemaphoreType.DMA((2,))],
-        compiler_params=pltpu.CompilerParams(vmem_limit_bytes=VMEM_ALL),
+        compiler_params=pltpu.CompilerParams(vmem_limit_bytes=VMEM_LIMIT),
         cost_estimate=pl.CostEstimate(flops=8000000, bytes_accessed=3000000, transcendentals=130000),
         name="ends_pass",
-    )(velocity, before, after, comp, table)
+    )(held, before, after, comp, table)
 
 
 def edge_kernel(edge_ref, ends_ref, lo_ref, hi_ref, comp_ref, tab_ref, mine_ref, other_ref):
@@ -327,13 +304,13 @@
 def local(velocity, sigma_table, color_table):
     layers, tiles = lax.axis_size("depth"), lax.axis_size("tile")
     table = make_table(sigma_table, color_table, velocity.shape[1] * layers)
-    up, down, zup, zdown = pack(velocity)
+    held, up, down, zup, zdown = pack(velocity)
     lo = lax.ppermute(up, "tile", ring(tiles, 1))
     hi = lax.ppermute(down, "tile", ring(tiles, -1))
     before = lax.ppermute(zup, "depth", ring(layers, 1))
     after = lax.ppermute(zdown, "depth", ring(layers, -1))
-    comp, edge = middle_pass(velocity, table)
-    comp, ends = ends_pass(velocity, before, after, comp, table)
+    comp, edge = middle_pass(held, table)
+    comp, ends = ends_pass(held, before, after, comp, table)
     mine, other = edge_pass(edge, ends, lo, hi, comp, table)
     return gather_over(mine, other)
 

time: 40.3 us -> 43.4 us (1.077)
  local copies, waits for them, and re-layouts: 0.16 us -> 6.44 us
  Pallas kernels: 19 us -> 15.9 us
    unnamed x4 -> x8, local copies, waits for them, and re-layouts: 0.01 us -> 6.29 us
    pallas_call x2, Pallas kernels: 13.6 us -> 10.5 us  [the longest x1 9.2 us: middle_pass(): pl.pallas_call(middle_kernel, out_shape=[jax.ShapeDtypeStruct((4, width,...]
  transfers between devices with their start and end apart: 8 -> 8, of which waited for: 4 -> 4; matrix products, arithmetic and copies ran while one was open for 1% -> 1% of each run, Pallas kernels for 34% -> 24%
where the time goes in v5:
time: 43.4 us; the launch traced here: 43.2 us
  Pallas kernels  15.9 us (37%)
  starting transfers between devices  15.3 us (35%)
  local copies, waits for them, and re-layouts  6.44 us (15%)
  waiting for transfers between devices  4.62 us (11%)
  other arithmetic  0.84 us (2%)
    pallas_call x1, Pallas kernels, middle_pass(): pl.pallas_call(middle_kernel, out_shape=[jax.ShapeDtypeStruct((4, width,...  9.2 us
    unnamed x8, local copies, waits for them, and re-layouts  6.29 us
    ppermute x3, starting transfers between devices, gather_over(): parts.append(lax.ppermute(piece, 'depth', ring(8, 2 * k)))  5.89 us
    ppermute x1, starting transfers between devices, local(): hi = lax.ppermute(down, 'tile', ring(tiles, -1))  4.74 us
    pallas_call x1, Pallas kernels, pack(): pl.pallas_call(pack_kernel, in_specs=[pl.BlockSpec(memory_space=pl.ANY)],...  4.04 us
    ppermute x1, starting transfers between devices, local(): after = lax.ppermute(zdown, 'depth', ring(layers, -1))  2.95 us
    ppermute x3, waiting for transfers between devices, gather_over(): parts.append(lax.ppermute(piece, 'depth', ring(8, 2 * k)))  2.56 us
    ppermute x1, starting transfers between devices, local(): lo = lax.ppermute(up, 'tile', ring(tiles, 1))  1.57 us
  transfers between devices with their start and end apart: 8, of which 4 were waited for; matrix products, arithmetic and copies ran while one was open for 1% of the time, Pallas kernels for 24%

profile of v5, /device:TPU:0, one launch (start us, length us, event | category | flops | bytes accessed | tf_op | source)
XLA Modules:
  0.0 43.2 jit_solution(3657716570117881863)
XLA Ops:
  0.0 0.0 copy-start.3
  0.0 0.0 copy-start.2
  0.0 4.0 %pack.1 = (f32[3,32,16,1280]{3,2,1,0:T(8,128)S(1)}, f32[3,8,8,1024]{3,2,1,0:T(8,128)}, f32[3,8,8,1024]{3,2,1,0:T(8,128)S(1)}, f32[3,2,16,1024]{3,2,1,0:T(8,128)}, f32[3,2,16,1024]{3,2,1,0:T(8,128)S(1)}) custom-call(f32[3,32,16,1024]{3,2,1,0:T(8,128)} %v_hbm.1), custom_call_target="tpu_custom_call" | custom-call | flops 2000000 | bytes 9000000 | tf_op jit(solution)/shard_map/pack/pallas_call | solution.py:62
  4.0 0.0 copy-start
  4.1 3.0 %copy-done = f32[3,32,16,1280]{3,2,1,0:T(8,128)} copy-done((f32[3,32,16,1280]{3,2,1,0:T(8,128)}, f32[3,32,16,1280]{3,2,1,0:T(8,128)S(1)}, u32[]{:S(2)}) %copy-start) | copy-done | bytes 7864344
  7.1 1.6 %collective-permute-start.2 = (f32[3,8,8,1024]{3,2,1,0:T(8,128)}, f32[3,8,8,1024]{3,2,1,0:T(8,128)S(1)}, u32[]{:S(2)}, u32[]{:S(2)}) collective-permute-start(f32[3,8,8,1024]{3,2,1,0:T(8,128)} %get-tuple-element.22), channel_id=1, source_target_pairs={{0,1},{1,2},{2,3},{3,4},{4,5},{5,6},{6,7},{7,8},{8,9},{9,10},{10,1... | collective-permute-start | bytes 2359304 | tf_op jit(solution)/shard_map/ppermute | solution.py:308
  8.7 4.7 %collective-permute-start.3 = (f32[3,8,8,1024]{3,2,1,0:T(8,128)S(1)}, f32[3,8,8,1024]{3,2,1,0:T(8,128)S(1)}, u32[]{:S(2)}, u32[]{:S(2)}) collective-permute-start(f32[3,8,8,1024]{3,2,1,0:T(8,128)S(1)} %get-tuple-element.23), channel_id=1, source_target_pairs={{0,15},{1,0},{2,1},{3,2},{4,3},{5,4},{6,5},{7,6},{8,7},{9,8},{10,9... | collective-permute-start | bytes 2359304 | tf_op jit(solution)/shard_map/ppermute | solution.py:309
  13.4 0.0 collective-permute-start
  13.4 3.0 %collective-permute-start.1 = (f32[3,2,16,1024]{3,2,1,0:T(8,128)S(1)}, f32[3,2,16,1024]{3,2,1,0:T(8,128)S(1)}, u32[]{:S(2)}, u32[]{:S(2)}) collective-permute-start(f32[3,2,16,1024]{3,2,1,0:T(8,128)S(1)} %get-tuple-element.19), channel_id=1, source_target_pairs={{0,112},{16,0},{32,16},{48,32},{64,48},{80,64},{96,80},{112,96},{1... | collective-permute-start | bytes 1179656 | tf_op jit(solution)/shard_map/ppermute | solution.py:311
  16.4 0.0 copy-done.3
  16.4 0.0 copy-done.2
  16.4 0.1 multiply_subtract_fusion
  16.5 0.1 broadcast_in_dim.4
  16.6 0.1 broadcast_in_dim.10.tab_ref
  16.6 0.0 copy-start.1
  16.6 3.2 %copy-done.1 = f32[3,32,16,1280]{3,2,1,0:T(8,128)S(1)} copy-done((f32[3,32,16,1280]{3,2,1,0:T(8,128)S(1)}, f32[3,32,16,1280]{3,2,1,0:T(8,128)}, u32[]{:S(2)}) %copy-start.1) | copy-done | bytes 7864344
  19.9 9.2 %middle_pass.1 = (f32[4,16,1024]{2,1,0:T(8,128)S(1)}, f32[4,2,8,8,1024]{4,3,2,1,0:T(8,128)S(1)}) custom-call(f32[3,32,16,1280]{3,2,1,0:T(8,128)S(1)} %copy-done.1, f32[16,8,128]{2,1,0:T(8,128)S(1)} %broadcast_in_dim.10.tab_ref), custom_call_target="tpu_custom_call" | custom-call | flops 60000000 | bytes 10000000 | tf_op jit(solution)/shard_map/middle_pass/pallas_call | solution.py:164
  29.1 0.0 collective-permute-done.zlo_ref
  29.1 0.0 collective-permute-done.1.zhi_ref
  29.1 1.3 %ends_pass.1 = (f32[4,16,1024]{2,1,0:T(8,128)S(1)}, f32[4,2,2,8,1024]{4,3,2,1,0:T(8,128)S(1)}) custom-call(f32[3,32,16,1280]{3,2,1,0:T(8,128)S(1)} %copy-done.1, f32[3,2,16,1024]{3,2,1,0:T(8,128)S(1)} %collective-permute-done.zlo_ref, f32[3,2,16,1024]{3,2,1,0:T(8,128)S(1)} %collective-permute-done.1.zhi_ref, f32[4,16,1024]{2,1,0:T(8,128)S(1)} %get-tuple-element.20.comp_ref, ...), custom_call_target="tpu_custom_call" | custom-call | flops 8000000 | bytes 3000000 | tf_op jit(solution)/shard_map/ends_pass/pallas_call | solution.py:217
  30.4 0.8 %collective-permute-done.2.lo_ref = f32[3,8,8,1024]{3,2,1,0:T(8,128)S(1)} collective-permute-done((f32[3,8,8,1024]{3,2,1,0:T(8,128)}, f32[3,8,8,1024]{3,2,1,0:T(8,128)S(1)}, u32[]{:S(2)}, u32[]{:S(2)}) %collective-permute-start.2) | collective-permute-done | bytes 786464 | tf_op jit(solution)/shard_map/ppermute | solution.py:308
  31.2 0.0 collective-permute-done.3.hi_ref
  31.2 1.4 %edge_pass.1 = (f32[4,4,16,128]{3,2,1,0:T(8,128)S(1)}, f32[4,4,16,128]{3,2,1,0:T(8,128)S(1)}) custom-call(f32[4,2,8,8,1024]{4,3,2,1,0:T(8,128)S(1)} %get-tuple-element.17.edge_ref, f32[4,2,2,8,1024]{4,3,2,1,0:T(8,128)S(1)} %get-tuple-element.21.ends_ref, f32[3,8,8,1024]{3,2,1,0:T(8,128)S(1)} %collective-permute-done.2.lo_ref, ...), custom_call_target="tpu_custom_call" | custom-call | flops 10000000 | bytes 4000000 | tf_op jit(solution)/shard_map/edge_pass/pallas_call | solution.py:264
  32.5 0.1 collective-permute-start.4
  32.7 1.3 %collective-permute-done.4 = f32[4,4,16,128]{3,2,1,0:T(8,128)S(1)} collective-permute-done((f32[4,4,16,128]{3,2,1,0:T(8,128)S(1)}, f32[4,4,16,128]{3,2,1,0:T(8,128)S(1)}, u32[]{:S(2)}, u32[]{:S(2)}) %collective-permute-start.4) | collective-permute-done | bytes 131104 | tf_op jit(solution)/shard_map/ppermute | solution.py:281
  34.1 1.6 %collective-permute-start.5 = (f32[4,16,128]{2,1,0:T(8,128)S(1)}, f32[4,16,128]{2,1,0:T(8,128)S(1)}, u32[]{:S(2)}, u32[]{:S(2)}) collective-permute-start(f32[4,16,128]{2,1,0:T(8,128)S(1)} %get-tuple-element.36), channel_id=1, source_target_pairs={{0,32},{16,48},{32,64},{48,80},{64,96},{80,112},{96,0},{112,16},{1... | collective-permute-start | bytes 98312 | tf_op jit(solution)/shard_map/ppermute | solution.py:287
  35.7 2.9 %collective-permute-start.6 = (f32[4,16,128]{2,1,0:T(8,128)S(1)}, f32[4,16,128]{2,1,0:T(8,128)S(1)}, u32[]{:S(2)}, u32[]{:S(2)}) collective-permute-start(f32[4,16,128]{2,1,0:T(8,128)S(1)} %get-tuple-element.37), channel_id=1, source_target_pairs={{0,64},{16,80},{32,96},{48,112},{64,0},{80,16},{96,32},{112,48},{1... | collective-permute-start | bytes 98312 | tf_op jit(solution)/shard_map/ppermute | solution.py:287
  38.6 1.3 %collective-permute-start.7 = (f32[4,16,128]{2,1,0:T(8,128)S(1)}, f32[4,16,128]{2,1,0:T(8,128)S(1)}, u32[]{:S(2)}, u32[]{:S(2)}) collective-permute-start(f32[4,16,128]{2,1,0:T(8,128)S(1)} %get-tuple-element.38), channel_id=1, source_target_pairs={{0,96},{16,112},{32,0},{48,16},{64,32},{80,48},{96,64},{112,80},{1... | collective-permute-start | bytes 98312 | tf_op jit(solution)/shard_map/ppermute | solution.py:287
  40.0 0.0 collective-permute-done.5
  40.0 1.2 %collective-permute-done.6 = f32[4,16,128]{2,1,0:T(8,128)S(1)} collective-permute-done((f32[4,16,128]{2,1,0:T(8,128)S(1)}, f32[4,16,128]{2,1,0:T(8,128)S(1)}, u32[]{:S(2)}, u32[]{:S(2)}) %collective-permute-start.6) | collective-permute-done | bytes 32800 | tf_op jit(solution)/shard_map/ppermute | solution.py:287
  41.1 1.4 %collective-permute-done.7 = f32[4,16,128]{2,1,0:T(8,128)S(1)} collective-permute-done((f32[4,16,128]{2,1,0:T(8,128)S(1)}, f32[4,16,128]{2,1,0:T(8,128)S(1)}, u32[]{:S(2)}, u32[]{:S(2)}) %collective-permute-start.7) | collective-permute-done | bytes 32800 | tf_op jit(solution)/shard_map/ppermute | solution.py:287
  42.6 0.6 %pad_maximum_fusion.1 = f32[4,16,128]{2,1,0:T(8,128)} fusion(f32[1,16,128]{2,1,0:T(8,128)S(1)} %get-tuple-element.32, f32[3,16,128]{2,1,0:T(8,128)S(1)} %fusion.13), kind=kLoop, calls=%fused_computation.21 | loop fusion | flops 8192 | bytes 65536 | tf_op jit(solution)/shard_map/concatenate | solution.py:275
  (10 shorter events, 0.1 us)
Async XLA Ops:
  0.0 16.4 %copy-start.3 = (f32[16]{0:T(128)S(1)}, f32[16]{0:T(128)}, u32[]{:S(2)}) copy-start(f32[16]{0:T(128)} %param.4) | copy-start | bytes 196
  0.0 16.4 %copy-start.2 = (f32[3,16]{1,0:T(4,128)S(1)}, f32[3,16]{1,0:T(4,128)}, u32[]{:S(2)}) copy-start(f32[3,16]{1,0:T(4,128)} %param.5) | copy-start | bytes 580
  4.0 3.0 %copy-start = (f32[3,32,16,1280]{3,2,1,0:T(8,128)}, f32[3,32,16,1280]{3,2,1,0:T(8,128)S(1)}, u32[]{:S(2)}) copy-start(f32[3,32,16,1280]{3,2,1,0:T(8,128)S(1)} %get-tuple-element.16.held_ref) | copy-start | bytes 23592964
  7.1 24.1 %collective-permute-start.2 = (f32[3,8,8,1024]{3,2,1,0:T(8,128)}, f32[3,8,8,1024]{3,2,1,0:T(8,128)S(1)}, u32[]{:S(2)}, u32[]{:S(2)}) collective-permute-start(f32[3,8,8,1024]{3,2,1,0:T(8,128)} %get-tuple-element.22), channel_id=1, source_target_pairs={{0,1},{1,2},{2,3},{3,4},{4,5},{5,6},{6,7},{7,8},{8,9},{9,10},{10,1... | collective-permute-start | bytes 2359304 | tf_op jit(solution)/shard_map/ppermute | solution.py:308
  8.7 22.5 %collective-permute-start.3 = (f32[3,8,8,1024]{3,2,1,0:T(8,128)S(1)}, f32[3,8,8,1024]{3,2,1,0:T(8,128)S(1)}, u32[]{:S(2)}, u32[]{:S(2)}) collective-permute-start(f32[3,8,8,1024]{3,2,1,0:T(8,128)S(1)} %get-tuple-element.23), channel_id=1, source_target_pairs={{0,15},{1,0},{2,1},{3,2},{4,3},{5,4},{6,5},{7,6},{8,7},{9,8},{10,9... | collective-permute-start | bytes 2359304 | tf_op jit(solution)/shard_map/ppermute | solution.py:309
  13.4 15.7 %collective-permute-start = (f32[3,2,16,1024]{3,2,1,0:T(8,128)}, f32[3,2,16,1024]{3,2,1,0:T(8,128)S(1)}, u32[]{:S(2)}, u32[]{:S(2)}) collective-permute-start(f32[3,2,16,1024]{3,2,1,0:T(8,128)} %get-tuple-element.18), channel_id=1, source_target_pairs={{0,16},{16,32},{32,48},{48,64},{64,80},{80,96},{96,112},{112,0},{1... | collective-permute-start | bytes 1179656 | tf_op jit(solution)/shard_map/ppermute | solution.py:310
  13.4 15.7 %collective-permute-start.1 = (f32[3,2,16,1024]{3,2,1,0:T(8,128)S(1)}, f32[3,2,16,1024]{3,2,1,0:T(8,128)S(1)}, u32[]{:S(2)}, u32[]{:S(2)}) collective-permute-start(f32[3,2,16,1024]{3,2,1,0:T(8,128)S(1)} %get-tuple-element.19), channel_id=1, source_target_pairs={{0,112},{16,0},{32,16},{48,32},{64,48},{80,64},{96,80},{112,96},{1... | collective-permute-start | bytes 1179656 | tf_op jit(solution)/shard_map/ppermute | solution.py:311
  16.6 3.2 %copy-start.1 = (f32[3,32,16,1280]{3,2,1,0:T(8,128)S(1)}, f32[3,32,16,1280]{3,2,1,0:T(8,128)}, u32[]{:S(2)}) copy-start(f32[3,32,16,1280]{3,2,1,0:T(8,128)} %copy-done) | copy-start | bytes 23592964
  32.5 1.4 %collective-permute-start.4 = (f32[4,4,16,128]{3,2,1,0:T(8,128)S(1)}, f32[4,4,16,128]{3,2,1,0:T(8,128)S(1)}, u32[]{:S(2)}, u32[]{:S(2)}) collective-permute-start(f32[4,4,16,128]{3,2,1,0:T(8,128)S(1)} %get-tuple-element.26), channel_id=1, source_target_pairs={{0,16},{16,0},{32,48},{48,32},{64,80},{80,64},{96,112},{112,96},{1... | collective-permute-start | bytes 393224 | tf_op jit(solution)/shard_map/ppermute | solution.py:281
  34.1 5.9 %collective-permute-start.5 = (f32[4,16,128]{2,1,0:T(8,128)S(1)}, f32[4,16,128]{2,1,0:T(8,128)S(1)}, u32[]{:S(2)}, u32[]{:S(2)}) collective-permute-start(f32[4,16,128]{2,1,0:T(8,128)S(1)} %get-tuple-element.36), channel_id=1, source_target_pairs={{0,32},{16,48},{32,64},{48,80},{64,96},{80,112},{96,0},{112,16},{1... | collective-permute-start | bytes 98312 | tf_op jit(solution)/shard_map/ppermute | solution.py:287
  35.7 5.4 %collective-permute-start.6 = (f32[4,16,128]{2,1,0:T(8,128)S(1)}, f32[4,16,128]{2,1,0:T(8,128)S(1)}, u32[]{:S(2)}, u32[]{:S(2)}) collective-permute-start(f32[4,16,128]{2,1,0:T(8,128)S(1)} %get-tuple-element.37), channel_id=1, source_target_pairs={{0,64},{16,80},{32,96},{48,112},{64,0},{80,16},{96,32},{112,48},{1... | collective-permute-start | bytes 98312 | tf_op jit(solution)/shard_map/ppermute | solution.py:287
  38.6 3.9 %collective-permute-start.7 = (f32[4,16,128]{2,1,0:T(8,128)S(1)}, f32[4,16,128]{2,1,0:T(8,128)S(1)}, u32[]{:S(2)}, u32[]{:S(2)}) collective-permute-start(f32[4,16,128]{2,1,0:T(8,128)S(1)} %get-tuple-element.38), channel_id=1, source_target_pairs={{0,96},{16,112},{32,0},{48,16},{64,32},{80,48},{96,64},{112,80},{1... | collective-permute-start | bytes 98312 | tf_op jit(solution)/shard_map/ppermute | solution.py:287

commit v6 on v4

--- a/solution.py
+++ b/solution.py
@@ -113,7 +113,7 @@
     return total, 2.0 * dz[1], 2.0 * dx[1], 2.0 * dy[1]
 
 
-def middle_kernel(v_hbm, tab_ref, comp_ref, edge_ref, buf, sems):
+def middle_kernel(v_hbm, tab_ref, comp_ref, edge_ref, near_ref, far_ref, buf, sems):
     j = pl.program_id(0)
 
     def copy(k):
@@ -138,12 +138,14 @@
     left = pl.ds(pl.multiple_of(j * 128, 128), 128)
     mid = pl.ds(pl.multiple_of(j * 128 + 128, 128), 128)
     right = pl.ds(pl.multiple_of(j * 128 + 256, 128), 128)
+    near_ref[...] = buf[:, 0:4, :, mid]
+    far_ref[...] = buf[:, 28:32, :, mid]
     for side in range(2):
         rows = slice(8 * side, 8 * side + 8)
         others = slice(8 - 8 * side, 16 - 8 * side)
         zeros = jnp.zeros((8, 128), F32)
         carry = (zeros + 1.0, [zeros] * 3)
-        lines = [[buf[c, z, rows, mid] for z in range(32)] for c in range(3)]
+        lines = [[buf[c, i, rows, mid] for i in range(32)] for c in range(3)]
         for z in range(2, 30):
             quarter, zz = z // 8, z % 8
             dz, dx, dy = gradients(
@@ -167,17 +169,22 @@
 
 def middle_pass(velocity, table):
     comps, depth, width, length = velocity.shape
+    image = pl.BlockSpec((4, width, 128), lambda j: (0, 0, j))
     return pl.pallas_call(
         middle_kernel,
         grid=(8,),
         in_specs=[pl.BlockSpec(memory_space=pl.ANY), pl.BlockSpec((16, 8, 128), lambda j: (0, 0, 0))],
         out_specs=[
-            pl.BlockSpec((4, width, 128), lambda j: (0, 0, j)),
+            image,
             pl.BlockSpec((4, 2, 8, 8, 128), lambda j: (0, 0, 0, 0, j)),
+            pl.BlockSpec((comps, 4, width, 128), lambda j: (0, 0, 0, j)),
+            pl.BlockSpec((comps, 4, width, 128), lambda j: (0, 0, 0, j)),
         ],
         out_shape=[
             jax.ShapeDtypeStruct((4, width, length), F32),
             jax.ShapeDtypeStruct((4, 2, 8, 8, length), F32),
+            jax.ShapeDtypeStruct((comps, 4, width, length), F32),
+            jax.ShapeDtypeStruct((comps, 4, width, length), F32),
         ],
         scratch_shapes=[pltpu.VMEM((comps, depth, width, length + 256), F32), pltpu.SemaphoreType.DMA((8,))],
         compiler_params=pltpu.CompilerParams(vmem_limit_bytes=VMEM_ALL),
@@ -186,12 +193,7 @@
     )(velocity, table)
 
 
-def ends_kernel(v_hbm, zlo_ref, zhi_ref, comp_ref, tab_ref, out_ref, edge_ref, buf, sems):
-    copies = [pltpu.make_async_copy(v_hbm.at[:, 28 * k : 28 * k + 4], buf.at[k], sems.at[k]) for k in range(2)]
-    for copy in copies:
-        copy.start()
-    for copy in copies:
-        copy.wait()
+def ends_kernel(near_ref, far_ref, zlo_ref, zhi_ref, comp_ref, tab_ref, out_ref, edge_ref):
     masks = edge_masks()
     zeros = jnp.zeros((8, 128), F32)
     for j in range(8):
@@ -200,18 +202,18 @@
             rows = slice(8 * side, 8 * side + 8)
             others = slice(8 - 8 * side, 16 - 8 * side)
             carry = (zeros + 1.0, [zeros] * 3)
-            for k in range(2):
+            for k, block_ref in enumerate((near_ref, far_ref)):
                 first = [[zlo_ref[c, i, rows, lanes] for i in range(2)] for c in range(3)] if k == 0 else [[]] * 3
                 last = [[zhi_ref[c, i, rows, lanes] for i in range(2)] for c in range(3)] if k == 1 else [[]] * 3
-                lines = [first[c] + [buf[k, c, i, rows, lanes] for i in range(4)] + last[c] for c in range(3)]
+                lines = [first[c] + [block_ref[c, i, rows, lanes] for i in range(4)] + last[c] for c in range(3)]
                 for i in range(2):
                     at = i + 2 * k
                     sideways = lambda m: [
-                        buf[k, c, at, rows, m * 128 : m * 128 + 128] if 0 <= m < 8 else zeros for c in range(3)
+                        block_ref[c, at, rows, m * 128 : m * 128 + 128] if 0 <= m < 8 else zeros for c in range(3)
                     ]
                     dz, dx, dy = gradients(
                         [lines[c][i : i + 5] for c in range(3)],
-                        [buf[k, c, at, others, lanes] for c in range(3)],
+                        [block_ref[c, at, others, lanes] for c in range(3)],
                         sideways(j - 1),
                         sideways(j + 1),
                         side,
@@ -232,21 +234,18 @@
             out_ref[3, rows, lanes] = carry[0]
 
 
-def ends_pass(velocity, before, after, comp, table):
-    comps, depth, width, length = velocity.shape
-    vmem = pl.BlockSpec(memory_space=pltpu.VMEM)
+def ends_pass(near, far, before, after, comp, table):
+    width, length = comp.shape[1:]
     return pl.pallas_call(
         ends_kernel,
-        in_specs=[pl.BlockSpec(memory_space=pl.ANY)] + [vmem] * 4,
         out_shape=[
             jax.ShapeDtypeStruct((4, width, length), F32),
             jax.ShapeDtypeStruct((4, 2, 2, 8, length), F32),
         ],
-        scratch_shapes=[pltpu.VMEM((2, comps, 4, width, length), F32), pltpu.SemaphoreType.DMA((2,))],
-        compiler_params=pltpu.CompilerParams(vmem_limit_bytes=VMEM_ALL),
+        compiler_params=pltpu.CompilerParams(vmem_limit_bytes=VMEM_LIMIT),
         cost_estimate=pl.CostEstimate(flops=8000000, bytes_accessed=3000000, transcendentals=130000),
         name="ends_pass",
-    )(velocity, before, after, comp, table)
+    )(near, far, before, after, comp, table)
 
 
 def edge_kernel(edge_ref, ends_ref, lo_ref, hi_ref, comp_ref, tab_ref, mine_ref, other_ref):
@@ -332,8 +331,8 @@
     hi = lax.ppermute(down, "tile", ring(tiles, -1))
     before = lax.ppermute(zup, "depth", ring(layers, 1))
     after = lax.ppermute(zdown, "depth", ring(layers, -1))
-    comp, edge = middle_pass(velocity, table)
-    comp, ends = ends_pass(velocity, before, after, comp, table)
+    comp, edge, near, far = middle_pass(velocity, table)
+    comp, ends = ends_pass(near, far, before, after, comp, table)
     mine, other = edge_pass(edge, ends, lo, hi, comp, table)
     return gather_over(mine, other)
 

time: 40.3 us -> 40.3 us (level)
  Pallas kernels: 19 us -> 17.9 us
  waiting for transfers between devices: 4.65 us -> 5.71 us
    pallas_call x1, Pallas kernels: 2.67 us -> 1.28 us  [ends_pass(): pl.pallas_call(ends_kernel, out_shape=[jax.ShapeDtypeStruct((4, width, le...]
    ppermute x1, waiting for transfers between devices: 0.8 us -> 1.86 us  [local(): lo = lax.ppermute(up, 'tile', ring(tiles, 1))]
  transfers between devices with their start and end apart: 8 -> 8, of which waited for: 4 -> 4; matrix products, arithmetic and copies ran while one was open for 1% -> 1% of each run, Pallas kernels for 34% -> 31%
where the time goes in v6:
time: 40.3 us; the launch traced here: 40.2 us
  Pallas kernels  17.9 us (44%)
  starting transfers between devices  15.4 us (38%)
  waiting for transfers between devices  5.71 us (14%)
  other arithmetic  0.85 us (2%)
    pallas_call x1, Pallas kernels, middle_pass(): pl.pallas_call(middle_kernel, grid=(8,), in_specs=[pl.BlockSpec(memory_sp...  11.3 us
    ppermute x3, starting transfers between devices, gather_over(): parts.append(lax.ppermute(piece, 'depth', ring(8, 2 * k)))  5.89 us
    ppermute x1, starting transfers between devices, local(): hi = lax.ppermute(down, 'tile', ring(tiles, -1))  4.82 us
    pallas_call x1, Pallas kernels, pack(): pl.pallas_call(pack_kernel, in_specs=[pl.BlockSpec(memory_space=pl.ANY)],...  4 us
    ppermute x1, starting transfers between devices, local(): after = lax.ppermute(zdown, 'depth', ring(layers, -1))  2.95 us
    ppermute x3, waiting for transfers between devices, gather_over(): parts.append(lax.ppermute(piece, 'depth', ring(8, 2 * k)))  2.56 us
    ppermute x1, waiting for transfers between devices, local(): lo = lax.ppermute(up, 'tile', ring(tiles, 1))  1.86 us
    ppermute x1, starting transfers between devices, local(): lo = lax.ppermute(up, 'tile', ring(tiles, 1))  1.64 us
  transfers between devices with their start and end apart: 8, of which 4 were waited for; matrix products, arithmetic and copies ran while one was open for 1% of the time, Pallas kernels for 31%

profile of v6, /device:TPU:0, one launch (start us, length us, event | category | flops | bytes accessed | tf_op | source)
XLA Modules:
  0.0 40.2 jit_solution(9396258633156791766)
XLA Ops:
  0.0 0.0 copy-start.1
  0.0 0.0 copy-start
  0.0 4.0 %pack.1 = (f32[3,8,8,1024]{3,2,1,0:T(8,128)}, f32[3,8,8,1024]{3,2,1,0:T(8,128)S(1)}, f32[3,2,16,1024]{3,2,1,0:T(8,128)}, f32[3,2,16,1024]{3,2,1,0:T(8,128)S(1)}) custom-call(f32[3,32,16,1024]{3,2,1,0:T(8,128)} %v_hbm.3), custom_call_target="tpu_custom_call" | custom-call | flops 2000000 | bytes 9000000 | tf_op jit(solution)/shard_map/pack/pallas_call | solution.py:52
  4.0 1.6 %collective-permute-start.2 = (f32[3,8,8,1024]{3,2,1,0:T(8,128)}, f32[3,8,8,1024]{3,2,1,0:T(8,128)S(1)}, u32[]{:S(2)}, u32[]{:S(2)}) collective-permute-start(f32[3,8,8,1024]{3,2,1,0:T(8,128)} %get-tuple-element.24), channel_id=1, source_target_pairs={{0,1},{1,2},{2,3},{3,4},{4,5},{5,6},{6,7},{7,8},{8,9},{9,10},{10,1... | collective-permute-start | bytes 2359304 | tf_op jit(solution)/shard_map/ppermute | solution.py:330
  5.7 4.8 %collective-permute-start.3 = (f32[3,8,8,1024]{3,2,1,0:T(8,128)S(1)}, f32[3,8,8,1024]{3,2,1,0:T(8,128)S(1)}, u32[]{:S(2)}, u32[]{:S(2)}) collective-permute-start(f32[3,8,8,1024]{3,2,1,0:T(8,128)S(1)} %get-tuple-element.25), channel_id=1, source_target_pairs={{0,15},{1,0},{2,1},{3,2},{4,3},{5,4},{6,5},{7,6},{8,7},{9,8},{10,9... | collective-permute-start | bytes 2359304 | tf_op jit(solution)/shard_map/ppermute | solution.py:331
  10.5 0.0 collective-permute-start
  10.5 3.0 %collective-permute-start.1 = (f32[3,2,16,1024]{3,2,1,0:T(8,128)S(1)}, f32[3,2,16,1024]{3,2,1,0:T(8,128)S(1)}, u32[]{:S(2)}, u32[]{:S(2)}) collective-permute-start(f32[3,2,16,1024]{3,2,1,0:T(8,128)S(1)} %get-tuple-element.21), channel_id=1, source_target_pairs={{0,112},{16,0},{32,16},{48,32},{64,48},{80,64},{96,80},{112,96},{1... | collective-permute-start | bytes 1179656 | tf_op jit(solution)/shard_map/ppermute | solution.py:333
  13.4 0.0 copy-done.1
  13.4 0.0 copy-done
  13.5 0.1 multiply_subtract_fusion
  13.5 0.1 broadcast_in_dim.4
  13.6 0.1 broadcast_in_dim.10.tab_ref
  13.7 11.3 %middle_pass.1 = (f32[4,16,1024]{2,1,0:T(8,128)S(1)}, f32[4,2,8,8,1024]{4,3,2,1,0:T(8,128)S(1)}, f32[3,4,16,1024]{3,2,1,0:T(8,128)S(1)}, f32[3,4,16,1024]{3,2,1,0:T(8,128)S(1)}) custom-call(f32[3,32,16,1024]{3,2,1,0:T(8,128)} %v_hbm.3, f32[16,8,128]{2,1,0:T(8,128)S(1)} %broadcast_in_dim.10.tab_ref), custom_call_target="tpu_custom_call" | custom-call | flops 60000000 | bytes 10000000 | tf_op jit(solution)/shard_map/middle_pass/pallas_call | solution.py:173
  25.0 0.0 collective-permute-done.zlo_ref
  25.0 0.0 collective-permute-done.1.zhi_ref
  25.0 1.3 %ends_pass.1 = (f32[4,16,1024]{2,1,0:T(8,128)S(1)}, f32[4,2,2,8,1024]{4,3,2,1,0:T(8,128)S(1)}) custom-call(f32[3,4,16,1024]{3,2,1,0:T(8,128)S(1)} %get-tuple-element.18.near_ref, f32[3,4,16,1024]{3,2,1,0:T(8,128)S(1)} %get-tuple-element.19.far_ref, f32[3,2,16,1024]{3,2,1,0:T(8,128)S(1)} %collective-permute-done.zlo_ref, ...), custom_call_target="tpu_custom_call" | custom-call | flops 8000000 | bytes 3000000 | tf_op jit(solution)/shard_map/ends_pass/pallas_call | solution.py:239
  26.3 1.9 %collective-permute-done.2.lo_ref = f32[3,8,8,1024]{3,2,1,0:T(8,128)S(1)} collective-permute-done((f32[3,8,8,1024]{3,2,1,0:T(8,128)}, f32[3,8,8,1024]{3,2,1,0:T(8,128)S(1)}, u32[]{:S(2)}, u32[]{:S(2)}) %collective-permute-start.2) | collective-permute-done | bytes 786464 | tf_op jit(solution)/shard_map/ppermute | solution.py:330
  28.2 0.0 collective-permute-done.3.hi_ref
  28.2 1.4 %edge_pass.1 = (f32[4,4,16,128]{3,2,1,0:T(8,128)S(1)}, f32[4,4,16,128]{3,2,1,0:T(8,128)S(1)}) custom-call(f32[4,2,8,8,1024]{4,3,2,1,0:T(8,128)S(1)} %get-tuple-element.17.edge_ref, f32[4,2,2,8,1024]{4,3,2,1,0:T(8,128)S(1)} %get-tuple-element.23.ends_ref, f32[3,8,8,1024]{3,2,1,0:T(8,128)S(1)} %collective-permute-done.2.lo_ref, ...), custom_call_target="tpu_custom_call" | custom-call | flops 10000000 | bytes 4000000 | tf_op jit(solution)/shard_map/edge_pass/pallas_call | solution.py:286
  29.5 0.1 collective-permute-start.4
  29.7 1.3 %collective-permute-done.4 = f32[4,4,16,128]{3,2,1,0:T(8,128)S(1)} collective-permute-done((f32[4,4,16,128]{3,2,1,0:T(8,128)S(1)}, f32[4,4,16,128]{3,2,1,0:T(8,128)S(1)}, u32[]{:S(2)}, u32[]{:S(2)}) %collective-permute-start.4) | collective-permute-done | bytes 131104 | tf_op jit(solution)/shard_map/ppermute | solution.py:303
  31.1 1.6 %collective-permute-start.5 = (f32[4,16,128]{2,1,0:T(8,128)S(1)}, f32[4,16,128]{2,1,0:T(8,128)S(1)}, u32[]{:S(2)}, u32[]{:S(2)}) collective-permute-start(f32[4,16,128]{2,1,0:T(8,128)S(1)} %get-tuple-element.38), channel_id=1, source_target_pairs={{0,32},{16,48},{32,64},{48,80},{64,96},{80,112},{96,0},{112,16},{1... | collective-permute-start | bytes 98312 | tf_op jit(solution)/shard_map/ppermute | solution.py:309
  32.7 2.9 %collective-permute-start.6 = (f32[4,16,128]{2,1,0:T(8,128)S(1)}, f32[4,16,128]{2,1,0:T(8,128)S(1)}, u32[]{:S(2)}, u32[]{:S(2)}) collective-permute-start(f32[4,16,128]{2,1,0:T(8,128)S(1)} %get-tuple-element.39), channel_id=1, source_target_pairs={{0,64},{16,80},{32,96},{48,112},{64,0},{80,16},{96,32},{112,48},{1... | collective-permute-start | bytes 98312 | tf_op jit(solution)/shard_map/ppermute | solution.py:309
  35.6 1.3 %collective-permute-start.7 = (f32[4,16,128]{2,1,0:T(8,128)S(1)}, f32[4,16,128]{2,1,0:T(8,128)S(1)}, u32[]{:S(2)}, u32[]{:S(2)}) collective-permute-start(f32[4,16,128]{2,1,0:T(8,128)S(1)} %get-tuple-element.40), channel_id=1, source_target_pairs={{0,96},{16,112},{32,0},{48,16},{64,32},{80,48},{96,64},{112,80},{1... | collective-permute-start | bytes 98312 | tf_op jit(solution)/shard_map/ppermute | solution.py:309
  36.9 0.0 collective-permute-done.5
  37.0 1.2 %collective-permute-done.6 = f32[4,16,128]{2,1,0:T(8,128)S(1)} collective-permute-done((f32[4,16,128]{2,1,0:T(8,128)S(1)}, f32[4,16,128]{2,1,0:T(8,128)S(1)}, u32[]{:S(2)}, u32[]{:S(2)}) %collective-permute-start.6) | collective-permute-done | bytes 32800 | tf_op jit(solution)/shard_map/ppermute | solution.py:309
  38.1 1.4 %collective-permute-done.7 = f32[4,16,128]{2,1,0:T(8,128)S(1)} collective-permute-done((f32[4,16,128]{2,1,0:T(8,128)S(1)}, f32[4,16,128]{2,1,0:T(8,128)S(1)}, u32[]{:S(2)}, u32[]{:S(2)}) %collective-permute-start.7) | collective-permute-done | bytes 32800 | tf_op jit(solution)/shard_map/ppermute | solution.py:309
  39.6 0.6 %pad_maximum_fusion.1 = f32[4,16,128]{2,1,0:T(8,128)} fusion(f32[1,16,128]{2,1,0:T(8,128)S(1)} %get-tuple-element.34, f32[3,16,128]{2,1,0:T(8,128)S(1)} %fusion.13), kind=kLoop, calls=%fused_computation.21 | loop fusion | flops 8192 | bytes 65536 | tf_op jit(solution)/shard_map/concatenate | solution.py:297
  (10 shorter events, 0.2 us)
Async XLA Ops:
  0.0 13.4 %copy-start.1 = (f32[16]{0:T(128)S(1)}, f32[16]{0:T(128)}, u32[]{:S(2)}) copy-start(f32[16]{0:T(128)} %param.4) | copy-start | bytes 196
  0.0 13.4 %copy-start = (f32[3,16]{1,0:T(4,128)S(1)}, f32[3,16]{1,0:T(4,128)}, u32[]{:S(2)}) copy-start(f32[3,16]{1,0:T(4,128)} %param.5) | copy-start | bytes 580
  4.0 24.1 %collective-permute-start.2 = (f32[3,8,8,1024]{3,2,1,0:T(8,128)}, f32[3,8,8,1024]{3,2,1,0:T(8,128)S(1)}, u32[]{:S(2)}, u32[]{:S(2)}) collective-permute-start(f32[3,8,8,1024]{3,2,1,0:T(8,128)} %get-tuple-element.24), channel_id=1, source_target_pairs={{0,1},{1,2},{2,3},{3,4},{4,5},{5,6},{6,7},{7,8},{8,9},{9,10},{10,1... | collective-permute-start | bytes 2359304 | tf_op jit(solution)/shard_map/ppermute | solution.py:330
  5.7 22.5 %collective-permute-start.3 = (f32[3,8,8,1024]{3,2,1,0:T(8,128)S(1)}, f32[3,8,8,1024]{3,2,1,0:T(8,128)S(1)}, u32[]{:S(2)}, u32[]{:S(2)}) collective-permute-start(f32[3,8,8,1024]{3,2,1,0:T(8,128)S(1)} %get-tuple-element.25), channel_id=1, source_target_pairs={{0,15},{1,0},{2,1},{3,2},{4,3},{5,4},{6,5},{7,6},{8,7},{9,8},{10,9... | collective-permute-start | bytes 2359304 | tf_op jit(solution)/shard_map/ppermute | solution.py:331
  10.5 14.5 %collective-permute-start = (f32[3,2,16,1024]{3,2,1,0:T(8,128)}, f32[3,2,16,1024]{3,2,1,0:T(8,128)S(1)}, u32[]{:S(2)}, u32[]{:S(2)}) collective-permute-start(f32[3,2,16,1024]{3,2,1,0:T(8,128)} %get-tuple-element.20), channel_id=1, source_target_pairs={{0,16},{16,32},{32,48},{48,64},{64,80},{80,96},{96,112},{112,0},{1... | collective-permute-start | bytes 1179656 | tf_op jit(solution)/shard_map/ppermute | solution.py:332
  10.5 14.5 %collective-permute-start.1 = (f32[3,2,16,1024]{3,2,1,0:T(8,128)S(1)}, f32[3,2,16,1024]{3,2,1,0:T(8,128)S(1)}, u32[]{:S(2)}, u32[]{:S(2)}) collective-permute-start(f32[3,2,16,1024]{3,2,1,0:T(8,128)S(1)} %get-tuple-element.21), channel_id=1, source_target_pairs={{0,112},{16,0},{32,16},{48,32},{64,48},{80,64},{96,80},{112,96},{1... | collective-permute-start | bytes 1179656 | tf_op jit(solution)/shard_map/ppermute | solution.py:333
  29.5 1.4 %collective-permute-start.4 = (f32[4,4,16,128]{3,2,1,0:T(8,128)S(1)}, f32[4,4,16,128]{3,2,1,0:T(8,128)S(1)}, u32[]{:S(2)}, u32[]{:S(2)}) collective-permute-start(f32[4,4,16,128]{3,2,1,0:T(8,128)S(1)} %get-tuple-element.28), channel_id=1, source_target_pairs={{0,16},{16,0},{32,48},{48,32},{64,80},{80,64},{96,112},{112,96},{1... | collective-permute-start | bytes 393224 | tf_op jit(solution)/shard_map/ppermute | solution.py:303
  31.1 5.9 %collective-permute-start.5 = (f32[4,16,128]{2,1,0:T(8,128)S(1)}, f32[4,16,128]{2,1,0:T(8,128)S(1)}, u32[]{:S(2)}, u32[]{:S(2)}) collective-permute-start(f32[4,16,128]{2,1,0:T(8,128)S(1)} %get-tuple-element.38), channel_id=1, source_target_pairs={{0,32},{16,48},{32,64},{48,80},{64,96},{80,112},{96,0},{112,16},{1... | collective-permute-start | bytes 98312 | tf_op jit(solution)/shard_map/ppermute | solution.py:309
  32.7 5.4 %collective-permute-start.6 = (f32[4,16,128]{2,1,0:T(8,128)S(1)}, f32[4,16,128]{2,1,0:T(8,128)S(1)}, u32[]{:S(2)}, u32[]{:S(2)}) collective-permute-start(f32[4,16,128]{2,1,0:T(8,128)S(1)} %get-tuple-element.39), channel_id=1, source_target_pairs={{0,64},{16,80},{32,96},{48,112},{64,0},{80,16},{96,32},{112,48},{1... | collective-permute-start | bytes 98312 | tf_op jit(solution)/shard_map/ppermute | solution.py:309
  35.6 3.9 %collective-permute-start.7 = (f32[4,16,128]{2,1,0:T(8,128)S(1)}, f32[4,16,128]{2,1,0:T(8,128)S(1)}, u32[]{:S(2)}, u32[]{:S(2)}) collective-permute-start(f32[4,16,128]{2,1,0:T(8,128)S(1)} %get-tuple-element.40), channel_id=1, source_target_pairs={{0,96},{16,112},{32,0},{48,16},{64,32},{80,48},{96,64},{112,80},{1... | collective-permute-start | bytes 98312 | tf_op jit(solution)/shard_map/ppermute | solution.py:309

commit v7 on v6

--- a/solution.py
+++ b/solution.py
@@ -307,10 +307,13 @@
     for k in range(1, 4):
         piece = lax.dynamic_index_in_dim(pair, lax.rem(chip + k, 4), 0, keepdims=False)
         parts.append(lax.ppermute(piece, "depth", ring(8, 2 * k)))
-    parts = jnp.stack(parts)
-    result = lax.dynamic_index_in_dim(parts, lax.rem(chip + 1, 4), 0, keepdims=False)
+    def at(source):
+        turn = lax.rem(chip + 4 - source, 4)
+        return jnp.where(turn < 2, jnp.where(turn == 0, parts[0], parts[1]), jnp.where(turn == 2, parts[2], parts[3]))
+
+    result = at(3)
     for source in (2, 1, 0):
-        result = over(lax.dynamic_index_in_dim(parts, lax.rem(chip + 4 - source, 4), 0, keepdims=False), result)
+        result = over(at(source), result)
     return result
 
 

time: 40.3 us -> 40.3 us (level)
  no operation moved by 1% of the time
where the time goes in v7:
time: 40.3 us; the launch traced here: 40.2 us
  Pallas kernels  17.9 us (44%)
  starting transfers between devices  15.4 us (38%)
  waiting for transfers between devices  5.72 us (14%)
  other arithmetic  0.84 us (2%)
    pallas_call x1, Pallas kernels, middle_pass(): pl.pallas_call(middle_kernel, grid=(8,), in_specs=[pl.BlockSpec(memory_sp...  11.3 us
    ppermute x3, starting transfers between devices, gather_over(): parts.append(lax.ppermute(piece, 'depth', ring(8, 2 * k)))  5.89 us
    ppermute x1, starting transfers between devices, local(): hi = lax.ppermute(down, 'tile', ring(tiles, -1))  4.82 us
    pallas_call x1, Pallas kernels, pack(): pl.pallas_call(pack_kernel, in_specs=[pl.BlockSpec(memory_space=pl.ANY)],...  3.99 us
    ppermute x1, starting transfers between devices, local(): after = lax.ppermute(zdown, 'depth', ring(layers, -1))  2.95 us
    ppermute x3, waiting for transfers between devices, gather_over(): parts.append(lax.ppermute(piece, 'depth', ring(8, 2 * k)))  2.56 us
    ppermute x1, waiting for transfers between devices, local(): lo = lax.ppermute(up, 'tile', ring(tiles, 1))  1.86 us
    ppermute x1, starting transfers between devices, local(): lo = lax.ppermute(up, 'tile', ring(tiles, 1))  1.64 us
  transfers between devices with their start and end apart: 8, of which 4 were waited for; matrix products, arithmetic and copies ran while one was open for 1% of the time, Pallas kernels for 31%

profile of v7, /device:TPU:0, one launch (start us, length us, event | category | flops | bytes accessed | tf_op | source)
XLA Modules:
  0.0 40.2 jit_solution(12287782765113014520)
XLA Ops:
  0.0 0.0 copy-start.1
  0.0 0.0 copy-start
  0.0 4.0 %pack.1 = (f32[3,8,8,1024]{3,2,1,0:T(8,128)}, f32[3,8,8,1024]{3,2,1,0:T(8,128)S(1)}, f32[3,2,16,1024]{3,2,1,0:T(8,128)}, f32[3,2,16,1024]{3,2,1,0:T(8,128)S(1)}) custom-call(f32[3,32,16,1024]{3,2,1,0:T(8,128)} %v_hbm.3), custom_call_target="tpu_custom_call" | custom-call | flops 2000000 | bytes 9000000 | tf_op jit(solution)/shard_map/pack/pallas_call | solution.py:52
  4.0 1.6 %collective-permute-start.2 = (f32[3,8,8,1024]{3,2,1,0:T(8,128)}, f32[3,8,8,1024]{3,2,1,0:T(8,128)S(1)}, u32[]{:S(2)}, u32[]{:S(2)}) collective-permute-start(f32[3,8,8,1024]{3,2,1,0:T(8,128)} %get-tuple-element.24), channel_id=1, source_target_pairs={{0,1},{1,2},{2,3},{3,4},{4,5},{5,6},{6,7},{7,8},{8,9},{9,10},{10,1... | collective-permute-start | bytes 2359304 | tf_op jit(solution)/shard_map/ppermute | solution.py:333
  5.6 4.8 %collective-permute-start.3 = (f32[3,8,8,1024]{3,2,1,0:T(8,128)S(1)}, f32[3,8,8,1024]{3,2,1,0:T(8,128)S(1)}, u32[]{:S(2)}, u32[]{:S(2)}) collective-permute-start(f32[3,8,8,1024]{3,2,1,0:T(8,128)S(1)} %get-tuple-element.25), channel_id=1, source_target_pairs={{0,15},{1,0},{2,1},{3,2},{4,3},{5,4},{6,5},{7,6},{8,7},{9,8},{10,9... | collective-permute-start | bytes 2359304 | tf_op jit(solution)/shard_map/ppermute | solution.py:334
  10.5 0.0 collective-permute-start
  10.5 3.0 %collective-permute-start.1 = (f32[3,2,16,1024]{3,2,1,0:T(8,128)S(1)}, f32[3,2,16,1024]{3,2,1,0:T(8,128)S(1)}, u32[]{:S(2)}, u32[]{:S(2)}) collective-permute-start(f32[3,2,16,1024]{3,2,1,0:T(8,128)S(1)} %get-tuple-element.21), channel_id=1, source_target_pairs={{0,112},{16,0},{32,16},{48,32},{64,48},{80,64},{96,80},{112,96},{1... | collective-permute-start | bytes 1179656 | tf_op jit(solution)/shard_map/ppermute | solution.py:336
  13.4 0.0 copy-done.1
  13.4 0.0 copy-done
  13.4 0.1 multiply_subtract_fusion
  13.5 0.1 broadcast_in_dim.4
  13.6 0.1 broadcast_in_dim.10.tab_ref
  13.7 11.3 %middle_pass.1 = (f32[4,16,1024]{2,1,0:T(8,128)S(1)}, f32[4,2,8,8,1024]{4,3,2,1,0:T(8,128)S(1)}, f32[3,4,16,1024]{3,2,1,0:T(8,128)S(1)}, f32[3,4,16,1024]{3,2,1,0:T(8,128)S(1)}) custom-call(f32[3,32,16,1024]{3,2,1,0:T(8,128)} %v_hbm.3, f32[16,8,128]{2,1,0:T(8,128)S(1)} %broadcast_in_dim.10.tab_ref), custom_call_target="tpu_custom_call" | custom-call | flops 60000000 | bytes 10000000 | tf_op jit(solution)/shard_map/middle_pass/pallas_call | solution.py:173
  25.0 0.0 collective-permute-done.zlo_ref
  25.0 0.0 collective-permute-done.1.zhi_ref
  25.0 1.3 %ends_pass.1 = (f32[4,16,1024]{2,1,0:T(8,128)S(1)}, f32[4,2,2,8,1024]{4,3,2,1,0:T(8,128)S(1)}) custom-call(f32[3,4,16,1024]{3,2,1,0:T(8,128)S(1)} %get-tuple-element.18.near_ref, f32[3,4,16,1024]{3,2,1,0:T(8,128)S(1)} %get-tuple-element.19.far_ref, f32[3,2,16,1024]{3,2,1,0:T(8,128)S(1)} %collective-permute-done.zlo_ref, ...), custom_call_target="tpu_custom_call" | custom-call | flops 8000000 | bytes 3000000 | tf_op jit(solution)/shard_map/ends_pass/pallas_call | solution.py:239
  26.3 1.9 %collective-permute-done.2.lo_ref = f32[3,8,8,1024]{3,2,1,0:T(8,128)S(1)} collective-permute-done((f32[3,8,8,1024]{3,2,1,0:T(8,128)}, f32[3,8,8,1024]{3,2,1,0:T(8,128)S(1)}, u32[]{:S(2)}, u32[]{:S(2)}) %collective-permute-start.2) | collective-permute-done | bytes 786464 | tf_op jit(solution)/shard_map/ppermute | solution.py:333
  28.1 0.0 collective-permute-done.3.hi_ref
  28.1 1.4 %edge_pass.1 = (f32[4,4,16,128]{3,2,1,0:T(8,128)S(1)}, f32[4,4,16,128]{3,2,1,0:T(8,128)S(1)}) custom-call(f32[4,2,8,8,1024]{4,3,2,1,0:T(8,128)S(1)} %get-tuple-element.17.edge_ref, f32[4,2,2,8,1024]{4,3,2,1,0:T(8,128)S(1)} %get-tuple-element.23.ends_ref, f32[3,8,8,1024]{3,2,1,0:T(8,128)S(1)} %collective-permute-done.2.lo_ref, ...), custom_call_target="tpu_custom_call" | custom-call | flops 10000000 | bytes 4000000 | tf_op jit(solution)/shard_map/edge_pass/pallas_call | solution.py:286
  29.5 0.1 collective-permute-start.4
  29.7 1.3 %collective-permute-done.4 = f32[4,4,16,128]{3,2,1,0:T(8,128)S(1)} collective-permute-done((f32[4,4,16,128]{3,2,1,0:T(8,128)S(1)}, f32[4,4,16,128]{3,2,1,0:T(8,128)S(1)}, u32[]{:S(2)}, u32[]{:S(2)}) %collective-permute-start.4) | collective-permute-done | bytes 131104 | tf_op jit(solution)/shard_map/ppermute | solution.py:303
  31.0 1.6 %collective-permute-start.5 = (f32[4,16,128]{2,1,0:T(8,128)S(1)}, f32[4,16,128]{2,1,0:T(8,128)S(1)}, u32[]{:S(2)}, u32[]{:S(2)}) collective-permute-start(f32[4,16,128]{2,1,0:T(8,128)S(1)} %get-tuple-element.38), channel_id=1, source_target_pairs={{0,32},{16,48},{32,64},{48,80},{64,96},{80,112},{96,0},{112,16},{1... | collective-permute-start | bytes 98312 | tf_op jit(solution)/shard_map/ppermute | solution.py:309
  32.7 2.9 %collective-permute-start.6 = (f32[4,16,128]{2,1,0:T(8,128)S(1)}, f32[4,16,128]{2,1,0:T(8,128)S(1)}, u32[]{:S(2)}, u32[]{:S(2)}) collective-permute-start(f32[4,16,128]{2,1,0:T(8,128)S(1)} %get-tuple-element.39), channel_id=1, source_target_pairs={{0,64},{16,80},{32,96},{48,112},{64,0},{80,16},{96,32},{112,48},{1... | collective-permute-start | bytes 98312 | tf_op jit(solution)/shard_map/ppermute | solution.py:309
  35.6 1.3 %collective-permute-start.7 = (f32[4,16,128]{2,1,0:T(8,128)S(1)}, f32[4,16,128]{2,1,0:T(8,128)S(1)}, u32[]{:S(2)}, u32[]{:S(2)}) collective-permute-start(f32[4,16,128]{2,1,0:T(8,128)S(1)} %get-tuple-element.40), channel_id=1, source_target_pairs={{0,96},{16,112},{32,0},{48,16},{64,32},{80,48},{96,64},{112,80},{1... | collective-permute-start | bytes 98312 | tf_op jit(solution)/shard_map/ppermute | solution.py:309
  36.9 0.0 collective-permute-done.5
  36.9 1.2 %collective-permute-done.6 = f32[4,16,128]{2,1,0:T(8,128)S(1)} collective-permute-done((f32[4,16,128]{2,1,0:T(8,128)S(1)}, f32[4,16,128]{2,1,0:T(8,128)S(1)}, u32[]{:S(2)}, u32[]{:S(2)}) %collective-permute-start.6) | collective-permute-done | bytes 32800 | tf_op jit(solution)/shard_map/ppermute | solution.py:309
  38.1 1.4 %collective-permute-done.7 = f32[4,16,128]{2,1,0:T(8,128)S(1)} collective-permute-done((f32[4,16,128]{2,1,0:T(8,128)S(1)}, f32[4,16,128]{2,1,0:T(8,128)S(1)}, u32[]{:S(2)}, u32[]{:S(2)}) %collective-permute-start.7) | collective-permute-done | bytes 32800 | tf_op jit(solution)/shard_map/ppermute | solution.py:309
  39.6 0.6 %pad_maximum_fusion = f32[4,16,128]{2,1,0:T(8,128)} fusion(f32[1,16,128]{2,1,0:T(8,128)S(1)} %get-tuple-element.44, f32[3,16,128]{2,1,0:T(8,128)S(1)} %fusion.13), kind=kLoop, calls=%fused_computation.21 | loop fusion | flops 8192 | bytes 65536 | tf_op jit(solution)/shard_map/concatenate | solution.py:297
  (11 shorter events, 0.1 us)
Async XLA Ops:
  0.0 13.4 %copy-start.1 = (f32[16]{0:T(128)S(1)}, f32[16]{0:T(128)}, u32[]{:S(2)}) copy-start(f32[16]{0:T(128)} %param.4) | copy-start | bytes 196
  0.0 13.4 %copy-start = (f32[3,16]{1,0:T(4,128)S(1)}, f32[3,16]{1,0:T(4,128)}, u32[]{:S(2)}) copy-start(f32[3,16]{1,0:T(4,128)} %param.5) | copy-start | bytes 580
  4.0 24.1 %collective-permute-start.2 = (f32[3,8,8,1024]{3,2,1,0:T(8,128)}, f32[3,8,8,1024]{3,2,1,0:T(8,128)S(1)}, u32[]{:S(2)}, u32[]{:S(2)}) collective-permute-start(f32[3,8,8,1024]{3,2,1,0:T(8,128)} %get-tuple-element.24), channel_id=1, source_target_pairs={{0,1},{1,2},{2,3},{3,4},{4,5},{5,6},{6,7},{7,8},{8,9},{9,10},{10,1... | collective-permute-start | bytes 2359304 | tf_op jit(solution)/shard_map/ppermute | solution.py:333
  5.6 22.5 %collective-permute-start.3 = (f32[3,8,8,1024]{3,2,1,0:T(8,128)S(1)}, f32[3,8,8,1024]{3,2,1,0:T(8,128)S(1)}, u32[]{:S(2)}, u32[]{:S(2)}) collective-permute-start(f32[3,8,8,1024]{3,2,1,0:T(8,128)S(1)} %get-tuple-element.25), channel_id=1, source_target_pairs={{0,15},{1,0},{2,1},{3,2},{4,3},{5,4},{6,5},{7,6},{8,7},{9,8},{10,9... | collective-permute-start | bytes 2359304 | tf_op jit(solution)/shard_map/ppermute | solution.py:334
  10.5 14.5 %collective-permute-start = (f32[3,2,16,1024]{3,2,1,0:T(8,128)}, f32[3,2,16,1024]{3,2,1,0:T(8,128)S(1)}, u32[]{:S(2)}, u32[]{:S(2)}) collective-permute-start(f32[3,2,16,1024]{3,2,1,0:T(8,128)} %get-tuple-element.20), channel_id=1, source_target_pairs={{0,16},{16,32},{32,48},{48,64},{64,80},{80,96},{96,112},{112,0},{1... | collective-permute-start | bytes 1179656 | tf_op jit(solution)/shard_map/ppermute | solution.py:335
  10.5 14.5 %collective-permute-start.1 = (f32[3,2,16,1024]{3,2,1,0:T(8,128)S(1)}, f32[3,2,16,1024]{3,2,1,0:T(8,128)S(1)}, u32[]{:S(2)}, u32[]{:S(2)}) collective-permute-start(f32[3,2,16,1024]{3,2,1,0:T(8,128)S(1)} %get-tuple-element.21), channel_id=1, source_target_pairs={{0,112},{16,0},{32,16},{48,32},{64,48},{80,64},{96,80},{112,96},{1... | collective-permute-start | bytes 1179656 | tf_op jit(solution)/shard_map/ppermute | solution.py:336
  29.5 1.4 %collective-permute-start.4 = (f32[4,4,16,128]{3,2,1,0:T(8,128)S(1)}, f32[4,4,16,128]{3,2,1,0:T(8,128)S(1)}, u32[]{:S(2)}, u32[]{:S(2)}) collective-permute-start(f32[4,4,16,128]{3,2,1,0:T(8,128)S(1)} %get-tuple-element.28), channel_id=1, source_target_pairs={{0,16},{16,0},{32,48},{48,32},{64,80},{80,64},{96,112},{112,96},{1... | collective-permute-start | bytes 393224 | tf_op jit(solution)/shard_map/ppermute | solution.py:303
  31.0 5.9 %collective-permute-start.5 = (f32[4,16,128]{2,1,0:T(8,128)S(1)}, f32[4,16,128]{2,1,0:T(8,128)S(1)}, u32[]{:S(2)}, u32[]{:S(2)}) collective-permute-start(f32[4,16,128]{2,1,0:T(8,128)S(1)} %get-tuple-element.38), channel_id=1, source_target_pairs={{0,32},{16,48},{32,64},{48,80},{64,96},{80,112},{96,0},{112,16},{1... | collective-permute-start | bytes 98312 | tf_op jit(solution)/shard_map/ppermute | solution.py:309
  32.7 5.4 %collective-permute-start.6 = (f32[4,16,128]{2,1,0:T(8,128)S(1)}, f32[4,16,128]{2,1,0:T(8,128)S(1)}, u32[]{:S(2)}, u32[]{:S(2)}) collective-permute-start(f32[4,16,128]{2,1,0:T(8,128)S(1)} %get-tuple-element.39), channel_id=1, source_target_pairs={{0,64},{16,80},{32,96},{48,112},{64,0},{80,16},{96,32},{112,48},{1... | collective-permute-start | bytes 98312 | tf_op jit(solution)/shard_map/ppermute | solution.py:309
  35.6 3.9 %collective-permute-start.7 = (f32[4,16,128]{2,1,0:T(8,128)S(1)}, f32[4,16,128]{2,1,0:T(8,128)S(1)}, u32[]{:S(2)}, u32[]{:S(2)}) collective-permute-start(f32[4,16,128]{2,1,0:T(8,128)S(1)} %get-tuple-element.40), channel_id=1, source_target_pairs={{0,96},{16,112},{32,0},{48,16},{64,32},{80,48},{96,64},{112,80},{1... | collective-permute-start | bytes 98312 | tf_op jit(solution)/shard_map/ppermute | solution.py:309
